TPU v7x, 256 devices: a whole 4x4x8 slice. The times are simulated.
256 devices in a mesh: section: 2 (over core), ctx: 16 (over x, y), ch: 8 (over z).
Axes of the slice: x: 4, y: 4, z: 8, core: 2. Of those that a mesh axis runs over, the one named last changes fastest.
Arguments:
- mixer_input: bfloat16 [2, 3072, 16384], P('section', 'ctx', 'ch'), may hold values from -24 to 24
- gate_input: bfloat16 [2, 3072, 16384], P('section', 'ctx', 'ch'), may hold values from -6 to 6
- upstream_grad: bfloat16 [2, 3072, 16384], P('section', 'ctx', 'ch'), may hold values from -24 to 24
- x_weight: bfloat16 [2, 16384, 544], P('section', 'ch'), may hold values from -0.046875 to 0.046875
- step_weight: bfloat16 [2, 512, 16384], P('section', None, 'ch'), may hold values from -0.25 to 0.25
- step_bias: float32 [2, 16384], P('section', 'ch'), may hold values from -3 to 0
- decay_log: float32 [2, 16, 16384], P('section', None, 'ch'), may hold values from -9 to -2
- skip_gain: float32 [2, 16384], P('section', 'ch'), may hold values from 0.5 to 5
Outputs:
- handed_input: bfloat16 [2, 3072, 16384], P('section', 'ctx', 'ch')
- handed_gate: bfloat16 [2, 3072, 16384], P('section', 'ctx', 'ch')
- grad_x_weight: float32 [2, 16384, 544], P('section', ('ch', 'ctx'))
- grad_step_weight: float32 [2, 512, 16384], P('section', 'ctx', 'ch')
- grad_step_bias: float32 [2, 16384], P('section', 'ch')
- grad_decay_log: float32 [2, 16, 16384], P('section', None, 'ch')
- grad_skip_gain: float32 [2, 16384], P('section', 'ch')
All inputs are finite; a program needn't handle non-finite values.
Results may differ from a plain program's by a relative error of at most 0.0045.
The roundings to bfloat16 on the way count: a program that leaves them out, or rounds other values in their place, can miss the bound.
Values may be sent and summed in bfloat16 or wider, within the bound.
A program may use at most 192 MiB of HBM per device.

v0:
```python
import jax
import jax.numpy as jnp
from jax import lax
from jax.sharding import PartitionSpec as P

R = 512
N = 16
BLOCK = 16
BLOCKS = 12


def carried_in(part, axis, combine, identity, reverse):
    count = lax.axis_size(axis)
    place = lax.axis_index(axis)
    ahead = count - 1 - place if reverse else place
    gathered = jax.tree.map(lambda a: lax.all_gather(a, axis), part)
    state = jax.tree.map(lambda a, e: jnp.zeros_like(a) + jnp.asarray(e, a.dtype), part, identity)

    def one(lap, state):
        source = count - 1 - lap if reverse else lap
        return combine(
            state, jax.tree.map(lambda a: lax.dynamic_index_in_dim(a, source, 0, False), gathered)
        )

    return lax.fori_loop(0, ahead, one, state)


def passed_along(block, axis, distance):
    devices = range(lax.axis_size(axis))
    route = [(i - distance, i) for i in devices if i - distance in devices]
    return lax.ppermute(block, axis, route)


def to_blocks(values):
    shaped = values.reshape((BLOCKS, BLOCK) + values.shape[1:])
    return jnp.swapaxes(shaped, 0, 1)


def from_blocks(values):
    return jnp.swapaxes(values, 0, 1).reshape((BLOCKS * BLOCK,) + values.shape[2:])


def compose(earlier, later):
    return (later[0] * earlier[0], later[1] + later[0] * earlier[1])


def contract_rows(left, right):
    return lax.dot_general(
        left, right, (((0,), (0,)), ((), ())), preferred_element_type=jnp.float32
    )


def contract_cols(left, right):
    return lax.dot_general(
        left, right, (((1,), (1,)), ((), ())), preferred_element_type=jnp.float32
    )


def body(
    mixer_input, gate_input, upstream_grad, x_weight, step_weight, step_bias, decay_log, skip_gain
):
    signal_low = mixer_input[0]
    weight_x = x_weight[0]
    weight_step = step_weight[0]
    skip_row = skip_gain[0]
    channels = signal_low.shape[1]
    projected = lax.psum(jnp.dot(signal_low, weight_x, preferred_element_type=jnp.float32), "ch")
    step_low = projected[:, :R].astype(jnp.bfloat16)
    in_mat = projected[:, R : R + N]
    out_mat = projected[:, R + N :]
    step_pre = (
        jnp.dot(step_low, weight_step, preferred_element_type=jnp.float32) + step_bias[0][None, :]
    )
    step_size = jax.nn.softplus(step_pre)
    rates = -jnp.exp(decay_log[0])
    signal = signal_low.astype(jnp.float32)
    gate = gate_input[0].astype(jnp.float32)
    upstream = upstream_grad[0].astype(jnp.float32)
    gate_sigmoid = jax.nn.sigmoid(gate)
    seed = upstream * gate * gate_sigmoid
    step_blocks = to_blocks(step_size)
    drive_blocks = to_blocks(step_size * signal)
    in_blocks = to_blocks(in_mat)
    out_blocks = to_blocks(out_mat)
    seed_blocks = to_blocks(seed)
    cum_after = jnp.cumsum(step_blocks, axis=0)
    cum_before = cum_after - step_blocks
    block_sum = cum_after[-1]
    zeros_blocks = jnp.zeros((BLOCKS, N, channels), jnp.float32)
    zeros_state = jnp.zeros((N, channels), jnp.float32)

    def forward_step(running, inputs):
        step_row, drive_row, in_row = inputs
        updated = (
            jnp.exp(step_row[:, None, :] * rates[None]) * running
            + drive_row[:, None, :] * in_row[:, :, None]
        )
        return (updated, running)

    block_end, before_local = lax.scan(
        forward_step, zeros_blocks, (step_blocks, drive_blocks, in_blocks)
    )

    def backward_step(incoming, inputs):
        step_row, out_row, seed_row = inputs
        adjoint = out_row[:, :, None] * seed_row[:, None, :] + incoming
        return (jnp.exp(step_row[:, None, :] * rates[None]) * adjoint, None)

    block_start, _ = lax.scan(
        backward_step, zeros_blocks, (step_blocks, out_blocks, seed_blocks), reverse=True
    )
    block_decay = jnp.exp(block_sum[:, None, :] * rates[None])

    def chain_forward(running, inputs):
        decay_row, end_row = inputs
        return (decay_row * running + end_row, running)

    def chain_backward(running, inputs):
        decay_row, start_row = inputs
        return (start_row + decay_row * running, running)

    device_end, entry_zero = lax.scan(chain_forward, zeros_state, (block_decay, block_end))
    device_start, exit_zero = lax.scan(
        chain_backward, zeros_state, (block_decay, block_start), reverse=True
    )
    device_sum = jnp.sum(block_sum, axis=0)
    running_sum = jnp.cumsum(block_sum, axis=0)
    prior_sum = running_sum - block_sum
    later_sum = device_sum[None, :] - running_sum
    device_decay = jnp.exp(device_sum[None, :] * rates)
    identity = (jnp.ones_like(device_decay), jnp.zeros_like(device_end))
    _, entry_device = carried_in((device_decay, device_end), "ctx", compose, identity, False)
    _, exit_device = carried_in((device_decay, device_start), "ctx", compose, identity, True)
    entry_blocks = entry_zero + jnp.exp(prior_sum[:, None, :] * rates[None]) * entry_device[None]
    exit_blocks = exit_zero + jnp.exp(later_sum[:, None, :] * rates[None]) * exit_device[None]

    def final_step(carried, inputs):
        incoming, decay_total = carried
        step_row, drive_row, in_row, out_row, seed_row, before_row, cum_row = inputs
        decay_now = jnp.exp(step_row[:, None, :] * rates[None])
        previous = before_row + jnp.exp(cum_row[:, None, :] * rates[None]) * entry_blocks
        current = decay_now * previous + drive_row[:, None, :] * in_row[:, :, None]
        adjoint = out_row[:, :, None] * seed_row[:, None, :] + incoming
        scanned_row = jnp.sum(out_row[:, :, None] * current, axis=1)
        grad_out_row = jnp.sum(seed_row[:, None, :] * current, axis=2)
        grad_in_row = jnp.sum(adjoint * drive_row[:, None, :], axis=2)
        grad_drive_row = jnp.sum(adjoint * in_row[:, :, None], axis=1)
        pulled = adjoint * previous * decay_now
        grad_decay_row = jnp.sum(pulled * rates[None], axis=1)
        decay_total = decay_total + jnp.sum(pulled * step_row[:, None, :], axis=0)
        return (
            (decay_now * adjoint, decay_total),
            (scanned_row, grad_out_row, grad_in_row, grad_drive_row, grad_decay_row),
        )

    (_, rate_grad), per_token = lax.scan(
        final_step,
        (exit_blocks, zeros_state),
        (step_blocks, drive_blocks, in_blocks, out_blocks, seed_blocks, before_local, cum_before),
        reverse=True,
    )
    scanned = from_blocks(per_token[0])
    grad_out = from_blocks(per_token[1])
    grad_in = from_blocks(per_token[2])
    grad_drive = from_blocks(per_token[3])
    grad_decay_step = from_blocks(per_token[4])
    mixed = scanned + skip_row[None, :] * signal
    d_gate = upstream * mixed * gate_sigmoid * (1.0 + gate * (1.0 - gate_sigmoid))
    d_signal = grad_drive * step_size + skip_row[None, :] * seed
    d_step = grad_drive * signal + grad_decay_step
    d_pre = d_step * jax.nn.sigmoid(step_pre)
    pre_rounded = d_pre.astype(jnp.bfloat16)
    low_part = contract_cols(pre_rounded, weight_step)
    d_low, d_in, d_out = lax.psum((low_part, grad_in, grad_out), "ch")
    d_projected = jnp.concatenate([d_low, d_in, d_out], axis=1).astype(jnp.bfloat16)
    d_input = d_signal + contract_cols(d_projected, weight_x)
    grad_x = contract_rows(signal_low, d_projected)
    grad_step = contract_rows(step_low, pre_rounded)
    grad_x_part, grad_step_part = (
        lax.psum_scatter(grad_x, "ctx", scatter_dimension=0, tiled=True),
        lax.psum_scatter(grad_step, "ctx", scatter_dimension=0, tiled=True),
    )
    bias_grad, decay_grad, skip_grad = lax.psum(
        (jnp.sum(d_pre, axis=0), rate_grad * rates, jnp.sum(seed * signal, axis=0)), "ctx"
    )
    handed_input, handed_gate = passed_along(
        (d_input.astype(jnp.bfloat16), d_gate.astype(jnp.bfloat16)), "section", -1
    )
    return (
        handed_input[None],
        handed_gate[None],
        grad_x_part[None],
        grad_step_part[None],
        bias_grad[None],
        decay_grad[None],
        skip_grad[None],
    )


def solution(mesh):
    return jax.shard_map(
        body,
        mesh=mesh,
        in_specs=(
            P("section", "ctx", "ch"),
            P("section", "ctx", "ch"),
            P("section", "ctx", "ch"),
            P("section", "ch", None),
            P("section", None, "ch"),
            P("section", "ch"),
            P("section", None, "ch"),
            P("section", "ch"),
        ),
        out_specs=(
            P("section", "ctx", "ch"),
            P("section", "ctx", "ch"),
            P("section", ("ch", "ctx"), None),
            P("section", "ctx", "ch"),
            P("section", "ch"),
            P("section", None, "ch"),
            P("section", "ch"),
        ),
        check_vma=False,
    )
```

profile of v0, /device:TPU:2, one launch (start us, length us, event | category | flops | bytes accessed | tf_op | source)
XLA Modules:
  0.0 913.8 jit_solution(1143802445229935281)
XLA Ops:
  15.8 72.5 %all-reduce.6.cloned.1.call-done = f32[192,544]{1,0:T(8,128)} async-done(((f32[192,544]{1,0:T(8,128)}), f32[192,544]{1,0:T(8,128)}) %all-reduce.6.cloned.1.call-update) | async-done | bytes 417808 | tf_op jit(solution)/shard_map/psum | solution.py:67
  88.3 4.2 convert_multiply_fusion.3
  94.9 3.8 copy_bitcast_fusion
  101.2 115.8 %while.115 = (s32[]{:T(128)}, f32[12,16,2048]{2,1,0:T(8,128)}, f32[16,12,16,2048]{3,2,1,0:T(8,128)}, f32[16,12,2048]{2,1,0:T(8,128)}, f32[16,2048]{1,0:T(8,128)S...) while((s32[]{:T(128)}, f32[12,16,2048]{2,1,0:T(8,128)}, ...), condition=%wide.region_11.12_spmd.clone, body=%wide.region_10.11_spmd.clone.sunk | while | flops 2359299 | bytes 7015280 | solution.py:100
  110.2 3.0 multiply_add_fusion.6
  117.6 3.0 multiply_add_fusion.6
  125.1 3.0 multiply_add_fusion.6
  132.4 3.0 multiply_add_fusion.6
  139.9 3.0 multiply_add_fusion.6
  147.3 3.0 multiply_add_fusion.6
  154.7 3.0 multiply_add_fusion.6
  162.2 3.0 multiply_add_fusion.6
  176.9 3.0 multiply_add_fusion.6
  206.6 3.0 multiply_add_fusion.6
  219.8 20.7 %while.116 = (s32[]{:T(128)}, f32[16,2048]{1,0:T(8,128)S(1)}, f32[12,16,2048]{2,1,0:T(8,128)}, f32[12,16,2048]{2,1,0:T(8,128)}, f32[12,16,2048]{2,1,0:T(8,128)}, /*index=5*/s32[]{:T(128)}, s32[]{:T(128)}) while((s32[]{:T(128)}, f32[16,2048]{1,0:T(8,128)S(1)}, f32[12,16,2048]{2,1,0:T(8,128)}, f32[12,16,2048]{2,1,0:T(8,128)}, ...), condition=%wide.region_13.14_spmd.clone, body=%wide.region_12.13_spmd.clone.sunk | while | flops 131075 | bytes 787036 | solution.py:122
  241.2 72.8 %while.113 = (s32[]{:T(128)}, f32[12,16,2048]{2,1,0:T(8,128)}, f32[16,12,2048]{2,1,0:T(8,128)}, f32[16,2048]{1,0:T(8,128)S(1)}, f32[16,12,16]{2,1,0:T(8,128)}, /...) while((s32[]{:T(128)}, f32[12,16,2048]{2,1,0:T(8,128)}, ...), condition=%wide.region_3.4_spmd.clone, body=%wide.region_2.3_spmd.clone.sunk | while | flops 1966084 | bytes 3869051 | solution.py:109
  273.9 3.1 fusion.55
  315.4 20.7 %while.114 = (s32[]{:T(128)}, f32[16,2048]{1,0:T(8,128)S(1)}, f32[12,16,2048]{2,1,0:T(8,128)}, f32[12,16,2048]{2,1,0:T(8,128)}, f32[12,16,2048]{2,1,0:T(8,128)}, /*index=5*/s32[]{:T(128)}, s32[]{:T(128)}, s32[]{:T(128)}) while((s32[]{:T(128)}, f32[16,2048]{1,0:T(8,128)S(1)}, f32[12,16,2048]{2,1,0:T(8,128)}, ...), condition=%wide.region_5.6_spmd.clone, body=%wide.region_4.5_spmd.clone.sunk | while | flops 131076 | bytes 786548 | solution.py:123
  338.6 23.4 %all-gather.6.cloned.1.call-done = f32[16,16,2048]{2,1,0:T(8,128)} async-done(((f32[1,16,2048]{2,1,0:T(8,128)}), f32[16,16,2048]{2,1,0:T(8,128)}) %all-gather.6.cloned.1.call-update) | async-done | bytes 2097168 | tf_op jit(solution)/shard_map/all_gather | solution.py:16
  362.0 4.2 while.112
  366.3 47.7 %all-gather.8.cloned.1.call-done = f32[256,2048]{1,0:T(8,128)} async-done(((f32[16,2048]{1,0:T(8,128)}), f32[256,2048]{1,0:T(8,128)}) %all-gather.8.cloned.1.call-update) | async-done | bytes 2097168 | tf_op jit(solution)/shard_map/all_gather | solution.py:16
  414.0 11.9 %while.111 = (s32[]{:T(128)}, f32[16,2048]{1,0:T(8,128)S(1)}, s32[]{:T(128)}, f32[16,16,2048]{2,1,0:T(8,128)}, f32[16,16,2048]{2,1,0:T(8,128)}, /*index=5*/s32[]{:T(128)}, s32[]{:T(128)}, s32[]{:T(128)}, s32[]{:T(128)}) while((s32[]{:T(128)}, f32[16,2048]{1,0:T(8,128)S(1)}, s32[]{:T(128)}, f32[16,16,2048]{2,1,0:T(8,128)}, ...), condition=%wide.region_9.10_spmd, body=%wide.region_8.9_spmd.sunk | while | flops 65542 | bytes 524431 | solution.py:25
  425.9 4.3 multiply_add_fusion.3
  436.2 190.2 %while.117 = (s32[]{:T(128)}, f32[12,16,2048]{2,1,0:T(8,128)}, f32[16,2048]{1,0:T(8,128)S(1)}, f32[16,12,2048]{2,1,0:T(8,128)}, f32[16,12,16]{2,1,0:T(8,128)}, /...) while((s32[]{:T(128)}, f32[12,16,2048]{2,1,0:T(8,128)}, ...), condition=%wide.region_23.24_spmd.clone, body=%wide.region_16.23_spmd.clone.sunk | while | flops 9395844 | bytes 9133811 | solution.py:156
  441.3 4.8 multiply_reduce_fusion.7
  453.2 4.8 multiply_reduce_fusion.7
  465.1 4.8 multiply_reduce_fusion.7
  477.0 4.8 multiply_reduce_fusion.7
  488.9 4.8 multiply_reduce_fusion.7
  500.8 4.8 multiply_reduce_fusion.7
  512.7 4.8 multiply_reduce_fusion.7
  524.5 4.8 multiply_reduce_fusion.7
  536.4 4.8 multiply_reduce_fusion.7
  548.3 4.8 multiply_reduce_fusion.7
  560.2 4.8 multiply_reduce_fusion.7
  572.1 4.8 multiply_reduce_fusion.7
  584.0 4.8 multiply_reduce_fusion.7
  595.9 4.8 multiply_reduce_fusion.7
  607.8 4.8 multiply_reduce_fusion.7
  619.6 4.8 multiply_reduce_fusion.7
  626.4 3.8 copy.38
  635.2 5.6 fusion.44
  648.6 38.4 %all-reduce.9 = (bf16[192,16]{1,0:T(8,128)(2,1)S(1)}, bf16[192,16]{1,0:T(8,128)(2,1)S(1)}, bf16[192,512]{1,0:T(8,128)(2,1)}) all-reduce(f32[192,16]{1,0:T(8,128)} %bitcast.256, f32[192,16]{1,0:T(8,128)} %bitcast.255, f32[192,512]{1,0:T(8,128)S(1)} %fusion.12), channel_id=1, replica_groups=mesh['section'=2,'ctx'=16,'ch'=8] {'ch'}, use_global_device_ids=true, to_apply=%region_26.27 | all-reduce | flops 104448 | bytes 626688 | tf_op jit(solution)/shard_map/psum | solution.py:174
  687.0 3.7 convolution_bitcast_fusion
  691.7 3.2 fusion.5
  697.5 68.0 %all-reduce = (f32[1,2048]{1,0:T(1,128)}, f32[1,2048]{1,0:T(1,128)}) all-reduce(f32[1,2048]{1,0:T(1,128)S(1)} %bitcast.261, f32[1,2048]{1,0:T(1,128)S(1)} %bitcast.262), channel_id=1, replica_groups=mesh['section'=2,'ctx'=16,'ch'=8] {'ctx'}, use_global_device_ids=true, to_apply=%region_30.31 | all-reduce | flops 4096 | bytes 32768 | tf_op jit(solution)/shard_map/psum | solution.py:183
  765.5 49.3 %reduce-scatter.5.cloned.1.call-done = f32[32,2048]{1,0:T(8,128)} async-done(((f32[512,2048]{1,0:T(8,128)}), f32[32,2048]{1,0:T(8,128)}) %reduce-scatter.5.cloned.1.call-update) | async-done | bytes 262160 | tf_op jit(solution)/shard_map/reduce_scatter | solution.py:181
  814.7 87.4 %reduce-scatter.3.cloned.1.call-done = f32[128,544]{0,1:T(8,128)} async-done(((f32[2048,544]{0,1:T(8,128)}), f32[128,544]{0,1:T(8,128)}) %reduce-scatter.3.cloned.1.call-update) | async-done | bytes 278544 | tf_op jit(solution)/shard_map/reduce_scatter | solution.py:180
  (422 shorter events, 373.2 us)
Async XLA Ops:
  7.2 1.6 copy-start
  7.2 4.7 copy-start.7
  7.2 81.1 %all-reduce.6.cloned.1.call-start = ((), (), s32[]{:S(2)}) async-start(), calls=%async_computation.2 | async-start | bytes 983040 | tf_op jit(solution)/shard_map/psum | solution.py:67
  11.8 326.8 %all-gather.10.cloned.1.call-start = ((), (), s32[]{:S(2)}) async-start(), calls=%async_computation.8 | async-start | bytes 2228224 | tf_op jit(solution)/shard_map/all_gather | solution.py:16
  13.4 74.9 %copy-start.3 = (bf16[1,192,2048]{2,1,0:T(8,128)(2,1)S(1)}, bf16[1,192,2048]{2,1,0:T(8,128)(2,1)}, u32[]{:S(2)}) copy-start(bf16[1,192,2048]{2,1,0:T(8,128)(2,1)} %param.22) | copy-start | bytes 2359300
  13.4 74.9 %copy-start.19 = (f32[1,2048]{1,0:T(1,128)S(1)}, f32[1,2048]{1,0:T(1,128)}, u32[]{:S(2)}) copy-start(f32[1,2048]{1,0:T(1,128)} %param.27) | copy-start | bytes 24580
  94.8 3.8 copy-start.9
  94.9 122.2 %copy-start.10 = (f32[12,2048]{1,0:T(8,128)}, f32[12,2048]{1,0:T(8,128)S(1)}, u32[]{:S(2)}) copy-start(f32[12,2048]{1,0:T(8,128)S(1)} %get-tuple-element.1041) | copy-start | bytes 294916
  94.9 3.8 copy-start.14
  240.5 0.7 copy-start.2
  241.1 120.9 %all-gather.6.cloned.1.call-start = ((), (), s32[]{:S(2)}) async-start(), calls=%async_computation.3 | async-start | bytes 2228224 | tf_op jit(solution)/shard_map/all_gather | solution.py:16
  314.1 99.9 %all-gather.8.cloned.1.call-start = ((), (), s32[]{:S(2)}) async-start(), calls=%async_computation.7 | async-start | bytes 2228224 | tf_op jit(solution)/shard_map/all_gather | solution.py:16
  315.4 21.4 %copy-start.11 = (f32[12,2048]{1,0:T(8,128)S(1)}, f32[12,2048]{1,0:T(8,128)}, u32[]{:S(2)}) copy-start(f32[12,2048]{1,0:T(8,128)} %copy-done.10) | copy-start | bytes 294916
  336.1 0.7 copy-start.1
  336.8 428.7 %all-reduce.8.cloned.1.call-start = ((), (), s32[]{:S(2)}) async-start(), calls=%async_computation.6 | async-start | bytes 262144 | tf_op jit(solution)/shard_map/psum | solution.py:183
  626.4 3.8 copy-start.5
  630.2 2.1 copy-start.4
  632.3 2.1 copy-start.15
  632.3 2.8 copy-start.20
  635.1 179.6 %reduce-scatter.5.cloned.1.call-start = ((), (), s32[]{:S(2)}) async-start(), calls=%async_computation.5 | async-start | bytes 4456448 | tf_op jit(solution)/shard_map/reduce_scatter | solution.py:181
  635.1 6.5 copy-start.8
  640.8 0.9 copy-start.6
  644.5 3.5 copy-start.16
  644.5 257.6 %reduce-scatter.3.cloned.1.call-start = ((), (), s32[]{:S(2)}) async-start(), calls=%async_computation.4 | async-start | bytes 4734976 | tf_op jit(solution)/shard_map/reduce_scatter | solution.py:180
  644.5 2.7 copy-start.17
  690.8 0.9 copy-start.13
  691.7 4.5 copy-start.12
  694.9 70.6 %collective-permute-start = (bf16[192,2048]{1,0:T(8,128)(2,1)}, bf16[192,2048]{1,0:T(8,128)(2,1)}, u32[]{:S(2)}, u32[]{:S(2)}) collective-permute-start(bf16[192,2048]{1,0:T(8,128)(2,1)} %fusion.5), channel_id=1, source_target_pairs={{128,0},{129,1},{130,2},{131,3},{132,4},{133,5},{134,6},{135,7},{1... | collective-permute-start | bytes 2359304 | tf_op jit(solution)/shard_map/ppermute | solution.py:31
  696.2 69.3 %collective-permute-start.1 = (bf16[192,2048]{1,0:T(8,128)(2,1)S(1)}, bf16[192,2048]{1,0:T(8,128)(2,1)}, u32[]{:S(2)}, u32[]{:S(2)}) collective-permute-start(bf16[192,2048]{1,0:T(8,128)(2,1)S(1)} %copy-done.12), channel_id=1, source_target_pairs={{128,0},{129,1},{130,2},{131,3},{132,4},{133,5},{134,6},{135,7},{1... | collective-permute-start | bytes 2359304 | tf_op jit(solution)/shard_map/ppermute | solution.py:31
  902.1 4.2 copy-start.18
Sparse Core Ops, SparseCore 0:
  11.9 76.3 all-reduce.5
  241.3 47.9 all-gather.9
  314.2 47.7 all-gather.5
  364.6 49.3 all-gather.7
  635.2 93.0 all-reduce.7
  732.3 82.3 reduce-scatter.4
  819.4 82.6 reduce-scatter.2
where the time goes:
time: 921 us; the launch traced here: 914 us
  other arithmetic  286 us (31%)
  waiting for transfers between devices  280 us (30%)
  local copies, waits for them, and re-layouts  203 us (22%)
  blocking collectives  106 us (12%)
  matrix products  19.5 us (2%)
  between operations  14.4 us (2%)
    reduce_scatter x1, waiting for transfers between devices, body(): lax.psum_scatter(grad_x, 'ctx', scatter_dimension=0, tiled=True)  87.4 us
    reduce_sum x16, other arithmetic, final_step(): grad_out_row = jnp.sum(seed_row[:, None, :] * current, axis=2)  76.2 us
    psum x1, waiting for transfers between devices, body(): lax.psum(jnp.dot(signal_low, weight_x, preferred_element_type=jnp.float32...  72.5 us
    all_gather x3, waiting for transfers between devices, carried_in(): gathered = jax.tree.map(lambda a: lax.all_gather(a, axis), part)  71.1 us
    psum x1, blocking collectives, body(): lax.psum((jnp.sum(d_pre, axis=0), rate_grad * rates, jnp.sum(seed * signa...  68 us
    reduce_scatter x1, waiting for transfers between devices, body(): lax.psum_scatter(grad_step, 'ctx', scatter_dimension=0, tiled=True)  49.3 us
    add x16, other arithmetic, forward_step(): jnp.exp(step_row[:, None, :] * rates[None]) * running  46.5 us
    mul x16, other arithmetic, backward_step(): return (jnp.exp(step_row[:, None, :] * rates[None]) * adjoint, None)  45.7 us
  transfers between devices with their start and end apart: 9, of which 5 were waited for; matrix products, arithmetic and copies ran while one was open for 14% of the time, Pallas kernels for 0%

commit v1 on v0

v1 whole, which is shorter than its diff:
```python
import functools

import jax
import jax.numpy as jnp
from jax import lax
from jax.experimental import pallas as pl
from jax.experimental.pallas import tpu as pltpu
from jax.sharding import PartitionSpec as P

R = 512
N = 16
TOK = 192
STEPS = 24
ROWS = 8
TILE = 256
LANE = 128
HALVES = TILE // LANE
CHUNK = 4
LOG2E = 1.4426950408889634
VMEM_BYTES = 60 * 2**20
SIDE = 4
CTX = 16
CH = 8
PIECE = TOK // CH
WIDE = R + LANE
PACK = 40
SMALL = 24
MESH = pl.DeviceIdType.MESH
LN2 = 0.6931471805599453
F32 = jnp.float32
BF16 = jnp.bfloat16


def every(i):
    return pl.ds(i, ROWS, stride=STEPS)


def lanes(k):
    return slice(k * LANE, (k + 1) * LANE)


def by_lanes(ref, value):
    for k in range(HALVES):
        ref[k] = value[:, lanes(k)]


def joined(ref):
    return jnp.concatenate([ref[k] for k in range(HALVES)], axis=1)


def row_index():
    return lax.broadcasted_iota(jnp.int32, (ROWS, LANE), 0)


def spread_columns(io_ref, spread):
    def one(i, _):
        rows = io_ref[every(i), :]
        for n in range(2 * N):
            spread[i, n] = jnp.broadcast_to(rows[:, n : n + 1], (ROWS, LANE))
        return 0

    lax.fori_loop(0, STEPS, one, 0)


def scan_rows(decay, value, reverse):
    row = row_index()
    for k in (1, 2, 4):
        shift = ROWS - k if reverse else k
        inside = row < ROWS - k if reverse else row >= k
        value = value + decay * jnp.where(inside, pltpu.roll(value, shift, 0), 0.0)
        if k < 4:
            decay = decay * jnp.where(inside, pltpu.roll(decay, shift, 0), 1.0)
    return value


def first_pass(
    low_ref, io_ref, w_ref, bias_ref, dlog_ref, u_ref, z_ref, g_ref,
    step_ref, sig_ref, entry_ref, exit_ref, pack_ref, bsum_ref,
    spread, drive, seed, rates,
):
    @pl.when(pl.program_id(0) == 0)
    def _():
        spread_columns(io_ref, spread)

    pre = jnp.dot(low_ref[...], w_ref[...], preferred_element_type=F32) + bias_ref[...]
    step = jnp.maximum(pre, 0.0) + jnp.log1p(jnp.exp(-jnp.abs(pre)))
    sig_ref[...] = jax.nn.sigmoid(pre)
    z = z_ref[...].astype(F32)
    by_lanes(step_ref, step)
    by_lanes(drive, step * u_ref[...].astype(F32))
    by_lanes(seed, g_ref[...].astype(F32) * z * jax.nn.sigmoid(z))
    rates[...] = -LOG2E * jnp.exp(dlog_ref[...])
    row = row_index()

    total = jnp.zeros((ROWS, TILE), F32)
    for i in range(STEPS):
        total = total + jnp.concatenate([step_ref[k, every(i), :] for k in range(HALVES)], axis=1)
    bsum_ref[...] = total
    whole_sum = jnp.sum(total, axis=0, keepdims=True)
    for k in range(HALVES):
        pack_ref[k, 2 * N :, :] = jnp.broadcast_to(whole_sum[:, lanes(k)], (PACK - 2 * N, LANE))

    for c in range(N // CHUNK):
        pairs = [(n, k) for n in range(c * CHUNK, (c + 1) * CHUNK) for k in range(HALVES)]
        rate = [jnp.broadcast_to(rates[n : n + 1, lanes(k)], (ROWS, LANE)) for n, k in pairs]

        def one(i, carry):
            state, decay, start = carry
            st = [step_ref[k, every(i), :] for k in range(HALVES)]
            dr = [drive[k, every(i), :] for k in range(HALVES)]
            sd = [seed[k, every(i), :] for k in range(HALVES)]
            new_state, new_decay, new_start = [], [], []
            for p, (n, k) in enumerate(pairs):
                a = jnp.exp2(st[k] * rate[p])
                new_state.append(a * state[p] + dr[k] * spread[i, n])
                d = a * decay[p]
                new_decay.append(d)
                new_start.append(start[p] + d * (sd[k] * spread[i, N + n]))
            return tuple(new_state), tuple(new_decay), tuple(new_start)

        zero = tuple(jnp.zeros((ROWS, LANE), F32) for _ in pairs)
        ones = tuple(jnp.ones((ROWS, LANE), F32) for _ in pairs)
        state, decay, start = lax.fori_loop(0, STEPS, one, (zero, ones, zero), unroll=4)
        for p, (n, k) in enumerate(pairs):
            ends = scan_rows(decay[p], state[p], False)
            starts = scan_rows(decay[p], start[p], True)
            entry_ref[n, :, lanes(k)] = jnp.where(row >= 1, pltpu.roll(ends, 1, 0), 0.0)
            exit_ref[n, :, lanes(k)] = jnp.where(row < ROWS - 1, pltpu.roll(starts, ROWS - 1, 0), 0.0)
            pack_ref[k, n : n + 1, :] = ends[ROWS - 1 :, :]
            pack_ref[k, N + n : N + n + 1, :] = starts[:1, :]


def sum_before(value, reverse):
    row = lax.broadcasted_iota(jnp.int32, value.shape, 0)
    held = value
    for k in (1, 2, 4):
        shift = ROWS - k if reverse else k
        inside = row < ROWS - k if reverse else row >= k
        held = held + jnp.where(inside, pltpu.roll(held, shift, 0), 0.0)
    return held - value


def second_pass(
    low_ref, io_ref, w_ref, dlog_ref, skip_ref, u_ref, z_ref, g_ref, step_ref, sig_ref,
    entry_ref, exit_ref, bsum_ref, across_ref,
    dgate_ref, dsig_ref, part_ref, gstep_ref, small_ref,
    spread, sums, held, drive, seed, scanned, grad_drive, grad_decay, rates, by_token,
):
    tile = pl.program_id(0)

    @pl.when(tile == 0)
    def _():
        spread_columns(io_ref, spread)
        sums[...] = jnp.zeros_like(sums)
        part_ref[...] = jnp.zeros_like(part_ref)

    step = joined(step_ref)
    u = u_ref[...].astype(F32)
    z = z_ref[...].astype(F32)
    g = g_ref[...].astype(F32)
    gate_sig = jax.nn.sigmoid(z)
    by_lanes(drive, step * u)
    by_lanes(seed, g * z * gate_sig)
    rates[...] = -LOG2E * jnp.exp(dlog_ref[...])
    scanned[...] = jnp.zeros_like(scanned)
    grad_drive[...] = jnp.zeros_like(grad_drive)
    grad_decay[...] = jnp.zeros_like(grad_decay)
    prior = sum_before(bsum_ref[...], False)
    later = sum_before(bsum_ref[...], True)

    for c in range(N // CHUNK):
        numbers = range(c * CHUNK, (c + 1) * CHUNK)
        pairs = [(n, k) for n in numbers for k in range(HALVES)]
        rate = [jnp.broadcast_to(rates[n : n + 1, lanes(k)], (ROWS, LANE)) for n, k in pairs]

        def forward(i, state):
            st = [step_ref[k, every(i), :] for k in range(HALVES)]
            dr = [drive[k, every(i), :] for k in range(HALVES)]
            sd = [seed[k, every(i), :] for k in range(HALVES)]
            out = [scanned[k, every(i), :] for k in range(HALVES)]
            new = []
            for m, n in enumerate(numbers):
                b_in, b_out = spread[i, n], spread[i, N + n]
                d_out = sums[i, N + n]
                for k in range(HALVES):
                    p = m * HALVES + k
                    held[i, m, :, lanes(k)] = state[p]
                    now = jnp.exp2(st[k] * rate[p]) * state[p] + dr[k] * b_in
                    new.append(now)
                    out[k] = out[k] + b_out * now
                    d_out = d_out + sd[k] * now
                sums[i, N + n] = d_out
            for k in range(HALVES):
                scanned[k, every(i), :] = out[k]
            return tuple(new)

        state = tuple(
            entry_ref[n, :, lanes(k)]
            + jnp.exp2(prior[:, lanes(k)] * rate[p]) * across_ref[k, n : n + 1, :]
            for p, (n, k) in enumerate(pairs)
        )
        lax.fori_loop(0, STEPS, forward, state, unroll=4)

        def backward(j, carry):
            incoming, total = carry
            i = STEPS - 1 - j
            st = [step_ref[k, every(i), :] for k in range(HALVES)]
            dr = [drive[k, every(i), :] for k in range(HALVES)]
            sd = [seed[k, every(i), :] for k in range(HALVES)]
            g_drive = [grad_drive[k, every(i), :] for k in range(HALVES)]
            g_decay = [grad_decay[k, every(i), :] for k in range(HALVES)]
            new_in, new_total = [], []
            for m, n in enumerate(numbers):
                b_in, b_out = spread[i, n], spread[i, N + n]
                d_in = sums[i, n]
                for k in range(HALVES):
                    p = m * HALVES + k
                    adjoint = b_out * sd[k] + incoming[p]
                    passed = jnp.exp2(st[k] * rate[p]) * adjoint
                    pulled = passed * held[i, m, :, lanes(k)]
                    new_in.append(passed)
                    new_total.append(total[p] + pulled * st[k])
                    g_decay[k] = g_decay[k] + pulled * rate[p]
                    g_drive[k] = g_drive[k] + adjoint * b_in
                    d_in = d_in + adjoint * dr[k]
                sums[i, n] = d_in
            for k in range(HALVES):
                grad_drive[k, every(i), :] = g_drive[k]
                grad_decay[k, every(i), :] = g_decay[k]
            return tuple(new_in), tuple(new_total)

        incoming = tuple(
            exit_ref[n, :, lanes(k)]
            + jnp.exp2(later[:, lanes(k)] * rate[p]) * across_ref[k, N + n : N + n + 1, :]
            for p, (n, k) in enumerate(pairs)
        )
        zero = tuple(jnp.zeros((ROWS, LANE), F32) for _ in pairs)
        _, total = lax.fori_loop(0, STEPS, backward, (incoming, zero), unroll=4)
        for p, (n, k) in enumerate(pairs):
            small_ref[k, n : n + 1, :] = (
                jnp.sum(total[p], axis=0, keepdims=True) * rates[n : n + 1, lanes(k)] * LN2
            )

    skip = skip_ref[...]
    by_drive = joined(grad_drive)
    seeds = joined(seed)
    mixed = joined(scanned) + skip * u
    dgate_ref[...] = (g * mixed * gate_sig * (1.0 + z * (1.0 - gate_sig))).astype(BF16)
    dsig_ref[...] = by_drive * step + skip * seeds
    d_pre = (by_drive * u + joined(grad_decay) * LN2) * sig_ref[...]
    pre = d_pre.astype(BF16)
    bias_row = jnp.sum(d_pre, axis=0, keepdims=True)
    skip_row = jnp.sum(seeds * u, axis=0, keepdims=True)
    for k in range(HALVES):
        small_ref[k, N : N + 1, :] = bias_row[:, lanes(k)]
        small_ref[k, N + 1 : N + 2, :] = skip_row[:, lanes(k)]
        small_ref[k, N + 2 :, :] = jnp.zeros((SMALL - N - 2, LANE), F32)
    part_ref[:, :R] += lax.dot_general(
        pre, w_ref[...], (((1,), (1,)), ((), ())), preferred_element_type=F32
    )
    grad = lax.dot_general(
        low_ref[...], pre, (((0,), (0,)), ((), ())), preferred_element_type=F32
    ).astype(BF16)
    for x in range(SIDE):
        for y in range(SIDE):
            at = (x * SIDE + y) * 2 * 16
            gstep_ref[0, x, y // 2, y % 2] = grad[at : at + 16]
            gstep_ref[1, y, x // 2, x % 2] = grad[at + 16 : at + 32]

    @pl.when(tile == pl.num_programs(0) - 1)
    def _():
        column = lax.broadcasted_iota(jnp.int32, (ROWS, LANE), 1)

        def one(i, _):
            rows = jnp.zeros((ROWS, LANE), F32)
            for n in range(2 * N):
                rows = jnp.where(column == n, jnp.sum(sums[i, n], axis=1, keepdims=True), rows)
            by_token[every(i), :] = rows
            return 0

        lax.fori_loop(0, STEPS, one, 0)
        part_ref[:, R:] = by_token[...]


def whole(*shape):
    return pl.BlockSpec(shape, lambda j: (0,) * len(shape))


def tiled(*lead):
    return pl.BlockSpec(lead + (TILE,), lambda j: (0,) * len(lead) + (j,))


def stacked(rows):
    return pl.BlockSpec((HALVES, rows, LANE), lambda j: (j, 0, 0))


def run_first(low, io, weight, bias, dlog, u, z, g):
    ch = u.shape[1]
    f = lambda *s: jax.ShapeDtypeStruct(s, F32)
    return pl.pallas_call(
        first_pass,
        grid=(ch // TILE,),
        in_specs=[
            whole(TOK, R), whole(TOK, io.shape[1]), tiled(R), tiled(1), tiled(N),
            tiled(TOK), tiled(TOK), tiled(TOK),
        ],
        out_specs=[
            stacked(TOK), tiled(TOK), tiled(N, ROWS), tiled(N, ROWS), stacked(PACK), tiled(ROWS),
        ],
        out_shape=[
            f(ch // LANE, TOK, LANE), f(TOK, ch), f(N, ROWS, ch), f(N, ROWS, ch),
            f(ch // LANE, PACK, LANE), f(ROWS, ch),
        ],
        scratch_shapes=[
            pltpu.VMEM((STEPS, 2 * N, ROWS, LANE), F32),
            pltpu.VMEM((HALVES, TOK, LANE), F32),
            pltpu.VMEM((HALVES, TOK, LANE), F32),
            pltpu.VMEM((N, TILE), F32),
        ],
        compiler_params=pltpu.CompilerParams(vmem_limit_bytes=VMEM_BYTES),
        name="first_pass",
    )(low, io, weight, bias, dlog, u, z, g)


def run_second(low, io, weight, dlog, skip, u, z, g, step, sig, entry, leave, bsum, across):
    ch = u.shape[1]
    f = lambda *s: jax.ShapeDtypeStruct(s, F32)
    return pl.pallas_call(
        second_pass,
        grid=(ch // TILE,),
        in_specs=[
            whole(TOK, R), whole(TOK, io.shape[1]), tiled(R), tiled(N), tiled(1),
            tiled(TOK), tiled(TOK), tiled(TOK), stacked(TOK), tiled(TOK),
            tiled(N, ROWS), tiled(N, ROWS), tiled(ROWS), stacked(2 * N),
        ],
        out_specs=[
            tiled(TOK), tiled(TOK), whole(TOK, WIDE), tiled(2, SIDE, 2, 2, 16), stacked(SMALL),
        ],
        out_shape=[
            jax.ShapeDtypeStruct((TOK, ch), BF16), f(TOK, ch), f(TOK, WIDE),
            jax.ShapeDtypeStruct((2, SIDE, 2, 2, 16, ch), BF16), f(ch // LANE, SMALL, LANE),
        ],
        scratch_shapes=[
            pltpu.VMEM((STEPS, 2 * N, ROWS, LANE), F32),
            pltpu.VMEM((STEPS, 2 * N, ROWS, LANE), F32),
            pltpu.VMEM((STEPS, CHUNK, ROWS, TILE), F32),
        ]
        + [pltpu.VMEM((HALVES, TOK, LANE), F32)] * 5
        + [pltpu.VMEM((N, TILE), F32), pltpu.VMEM((TOK, LANE), F32)],
        compiler_params=pltpu.CompilerParams(vmem_limit_bytes=VMEM_BYTES),
        name="second_pass",
    )(low, io, weight, dlog, skip, u, z, g, step, sig, entry, leave, bsum, across)


def greet(partners):
    barrier = pltpu.get_barrier_semaphore()
    for partner in partners:
        pl.semaphore_signal(barrier, inc=1, device_id=partner, device_id_type=MESH)
    pl.semaphore_wait(barrier, len(partners))


def remote(src, dst, send, recv, to):
    return pltpu.make_async_remote_copy(
        src_ref=src, dst_ref=dst, send_sem=send, recv_sem=recv, device_id=to, device_id_type=MESH
    )


def others(axis, count):
    me = lax.axis_index(axis)
    return [{axis: lax.rem(me + d, count)} for d in range(1, count)]


def token_rows(owner):
    return pl.ds(pl.multiple_of(owner * PIECE, 8), PIECE)


def sum_start(part_ref, landed, send, recv):
    copies = []
    for d, to in enumerate(others("ch", CH)):
        copies.append(remote(part_ref.at[token_rows(to["ch"])], landed.at[d], send.at[d], recv.at[d], to))
        copies[-1].start()
    return copies


def sum_finish(copies, part_ref, landed):
    me = lax.axis_index("ch")
    for copy in copies:
        copy.wait_recv()
    total = part_ref[token_rows(me), :]
    for d in range(CH - 1):
        total = total + landed[d]
    return total


def share_start(total, low_all, io_all, send, recv):
    me = lax.axis_index("ch")
    low_all[me] = jnp.concatenate([total[:, : R // 2], total[:, R // 2 : R]], axis=0).astype(BF16)
    io_all[me] = total[:, R:]
    copies = []
    for d, to in enumerate(others("ch", CH)):
        copies.append(remote(low_all.at[me], low_all.at[me], send.at[0, d], recv.at[0, d], to))
        copies.append(remote(io_all.at[me], io_all.at[me], send.at[1, d], recv.at[1, d], to))
    for copy in copies:
        copy.start()
    return copies


def share_finish(copies, low_all, io_all, wide):
    for copy in copies:
        copy.wait_recv()
    for p in range(CH):
        both = low_all[p].astype(F32)
        rows = slice(p * PIECE, (p + 1) * PIECE)
        wide[rows, : R // 2] = both[:PIECE]
        wide[rows, R // 2 : R] = both[PIECE:]
        wide[rows, R:] = io_all[p]


SUM_SCRATCH = [
    pltpu.VMEM((CH - 1, PIECE, WIDE), F32),
    pltpu.VMEM((CH, 2 * PIECE, R // 2), BF16),
    pltpu.VMEM((CH, PIECE, LANE), F32),
    pltpu.VMEM((TOK, WIDE), F32),
    pltpu.SemaphoreType.DMA((CH - 1,)),
    pltpu.SemaphoreType.DMA((CH - 1,)),
    pltpu.SemaphoreType.DMA((2, CH - 1)),
    pltpu.SemaphoreType.DMA((2, CH - 1)),
]


def sum_projected(
    part_ref, low_ref, io_ref, landed, low_all, io_all, wide, sum_send, sum_recv, all_send, all_recv
):
    greet(others("ch", CH))
    sums = sum_start(part_ref, landed, sum_send, sum_recv)
    shares = share_start(sum_finish(sums, part_ref, landed), low_all, io_all, all_send, all_recv)
    share_finish(shares, low_all, io_all, wide)
    low_ref[...] = wide[:, :R].astype(BF16)
    io_ref[...] = wide[:, R:]
    for copy in sums + shares:
        copy.wait_send()


def in_vmem(count):
    return [pl.BlockSpec(memory_space=pltpu.VMEM)] * count


def run_sum(part):
    return pl.pallas_call(
        sum_projected,
        in_specs=in_vmem(1),
        out_specs=in_vmem(2),
        out_shape=[jax.ShapeDtypeStruct((TOK, R), BF16), jax.ShapeDtypeStruct((TOK, LANE), F32)],
        scratch_shapes=SUM_SCRATCH,
        compiler_params=pltpu.CompilerParams(
            collective_id=0, has_side_effects=True, vmem_limit_bytes=VMEM_BYTES
        ),
        name="sum_projected",
    )(part)


def spread_start(src, dst, send, recv):
    me = lax.axis_index("ctx")
    copies = []
    for d, to in enumerate(others("ctx", CTX)):
        copies.append(remote(src.at[to["ctx"]], dst.at[me], send.at[d], recv.at[d], to))
        copies[-1].start()
    dst[me] = src[me]
    return copies


def exchange(pack_ref, dlog_ref, out_ref, landed, back, result, send, recv, back_send, back_recv):
    me = lax.axis_index("ctx")
    greet(others("ctx", CTX))
    there = spread_start(pack_ref, landed, send, recv)
    rates = -jnp.exp(dlog_ref[:, pl.ds(pl.multiple_of(me * LANE, LANE), LANE)])
    for copy in there:
        copy.wait_recv()
    state = jnp.zeros((N, LANE), F32)
    adjoint = jnp.zeros((N, LANE), F32)
    for c in range(CTX):
        r = CTX - 1 - c
        back[c, :N] = state
        back[r, N:] = adjoint
        state = jnp.exp(landed[c, 2 * N : 2 * N + 1] * rates) * state + landed[c, :N]
        adjoint = jnp.exp(landed[r, 2 * N : 2 * N + 1] * rates) * adjoint + landed[r, N : 2 * N]
    home = spread_start(back, result, back_send, back_recv)
    for copy in home:
        copy.wait_recv()
    out_ref[...] = result[...]
    for copy in there + home:
        copy.wait_send()


def run_exchange(pack, dlog):
    return pl.pallas_call(
        exchange,
        in_specs=in_vmem(2),
        out_specs=pl.BlockSpec(memory_space=pltpu.VMEM),
        out_shape=jax.ShapeDtypeStruct((CTX, 2 * N, LANE), F32),
        scratch_shapes=[
            pltpu.VMEM((CTX, PACK, LANE), F32),
            pltpu.VMEM((CTX, 2 * N, LANE), F32),
            pltpu.VMEM((CTX, 2 * N, LANE), F32),
        ]
        + [pltpu.SemaphoreType.DMA((CTX - 1,))] * 4,
        compiler_params=pltpu.CompilerParams(
            collective_id=1, has_side_effects=True, vmem_limit_bytes=VMEM_BYTES
        ),
        name="exchange",
    )(pack, dlog)


def neighbour(axis, d):
    me = lax.axis_index("ctx")
    x, y = me // SIDE, lax.rem(me, SIDE)
    if axis == 0:
        return {"ctx": lax.rem(x + d + SIDE, SIDE) * SIDE + y}
    return {"ctx": x * SIDE + lax.rem(y + d + SIDE, SIDE)}


def place(axis, d=0):
    me = lax.axis_index("ctx")
    at = me // SIDE if axis == 0 else lax.rem(me, SIDE)
    return lax.rem(at + d + SIDE, SIDE)


WAYS = ((0, 1, 0), (1, -1, 1))


def ring_start(axis, src, relay, land, send, recv):
    passing, direct = [], []
    for way, d, half in WAYS:
        to = neighbour(axis, d)
        passing.append(remote(src.at[place(axis, 2), half], relay.at[way], send.at[0, way], recv.at[0, way], to))
        direct.append(
            remote(src.at[place(axis, d), 1 - half], land.at[way, 1 - half], send.at[1, way], recv.at[1, way], to)
        )
        passing[-1].start()
    for copy in direct:
        copy.start()
    return passing, direct


def ring_middle(axis, src, relay, land, send, recv, copies):
    passing, direct = copies
    last = []
    for way, d, half in WAYS:
        passing[way].wait_recv()
        mine = src[place(axis, d), half]
        relay[way] = (relay[way].astype(F32) + mine.astype(F32)).astype(BF16)
        last.append(
            remote(relay.at[way], land.at[way, half], send.at[2, way], recv.at[2, way], neighbour(axis, d))
        )
        last[-1].start()
    return passing, direct, last


def ring_finish(axis, src, land, copies):
    _, direct, last = copies
    for copy in direct + last:
        copy.wait_recv()
    mine = place(axis)
    return [
        src[mine, h].astype(F32) + land[0, h].astype(F32) + land[1, h].astype(F32) for h in range(2)
    ]


def ring_done(copies):
    for group in copies:
        for copy in group:
            copy.wait_send()


def ring_scratch(unit, second):
    return [
        pltpu.VMEM((2, 2) + unit, BF16),
        pltpu.VMEM((2, 2, 2) + unit, BF16),
        pltpu.VMEM((2, SIDE, 2) + second, BF16),
        pltpu.VMEM((2, 2) + second, BF16),
        pltpu.VMEM((2, 2, 2) + second, BF16),
        pltpu.SemaphoreType.DMA((2, 3, 2)),
        pltpu.SemaphoreType.DMA((2, 3, 2)),
        pltpu.SemaphoreType.DMA((2, 3, 2)),
        pltpu.SemaphoreType.DMA((2, 3, 2)),
    ]


STEP_UNIT, STEP_SECOND = (2, 16, 2048), (16, 1024)
X_UNIT, X_SECOND = (2, 64, R + 2 * N), (32, R + 2 * N)


def plane_start(src, scratch):
    relay, land, _, _, _, send, recv, _, _ = scratch
    return [
        ring_start(q, src.at[q], relay.at[q], land.at[q], send.at[q], recv.at[q]) for q in range(2)
    ]


def plane_middle(src, scratch, copies):
    relay, land, _, _, _, send, recv, _, _ = scratch
    return [
        ring_middle(q, src.at[q], relay.at[q], land.at[q], send.at[q], recv.at[q], copies[q]) for q in range(2)
    ]


def plane_turn(src, scratch, copies, split):
    _, land, second, relay, land2, _, _, send, recv = scratch
    started = []
    for q in range(2):
        halves = ring_finish(q, src.at[q], land.at[q], copies[q])
        for o in range(SIDE):
            for h in range(2):
                second[q, o, h] = split(halves[o // 2][o % 2], h).astype(BF16)
        started.append(
            ring_start(1 - q, second.at[q], relay.at[q], land2.at[q], send.at[q], recv.at[q])
        )
    return started


def plane_second_middle(scratch, copies):
    _, _, second, relay, land, _, _, send, recv = scratch
    return [
        ring_middle(1 - q, second.at[q], relay.at[q], land.at[q], send.at[q], recv.at[q], copies[q])
        for q in range(2)
    ]


def plane_finish(scratch, copies):
    second, land = scratch[2], scratch[4]
    return [ring_finish(1 - q, second.at[q], land.at[q], copies[q]) for q in range(2)]


def tail(
    part_ref, small_in, dgate_ref, step_grad, u_ref, xw_ref, dsig_ref,
    hin_ref, hgate_ref, gx_ref, gstep_ref, small_ref,
    landed, low_all, io_all, wide, sum_send, sum_recv, all_send, all_recv,
    small_land, small_back, small_all, s_send, s_recv, t_send, t_recv,
    gate_land, in_out, in_land, hand_send, hand_recv, proj, x_grad, *rings,
):
    step_ring, x_ring = rings[:9], rings[9:]
    section = lax.axis_index("section")
    me = lax.axis_index("ctx")
    greet(others("ctx", CTX) + others("ch", CH) + [{"section": 1 - section}])
    gate_copy = remote(dgate_ref, gate_land, hand_send.at[0], hand_recv.at[0], {"section": 1 - section})
    in_copy = remote(in_out, in_land, hand_send.at[1], hand_recv.at[1], {"section": 1 - section})

    sums = sum_start(part_ref, landed, sum_send, sum_recv)
    first = plane_start(step_grad, step_ring)

    @pl.when(section == 1)
    def _():
        gate_copy.start()

    small_there = spread_start(small_in, small_land, s_send, s_recv)
    shares = share_start(sum_finish(sums, part_ref, landed), low_all, io_all, all_send, all_recv)
    first = plane_middle(step_grad, step_ring, first)
    for copy in small_there:
        copy.wait_recv()
    total = small_land[0]
    for c in range(1, CTX):
        total = total + small_land[c]
    small_all[me] = total
    small_home = []
    for d, to in enumerate(others("ctx", CTX)):
        small_home.append(remote(small_all.at[me], small_all.at[me], t_send.at[d], t_recv.at[d], to))
        small_home[-1].start()

    share_finish(shares, low_all, io_all, wide)
    proj[...] = wide[...].astype(BF16)

    def product(c, _):
        columns = pl.ds(pl.multiple_of(c * LANE, LANE), LANE)
        grad = lax.dot_general(
            u_ref[:, columns], proj[...], (((0,), (0,)), ((), ())), preferred_element_type=F32
        )[:, : R + 2 * N].astype(BF16)
        x, y = c // SIDE, lax.rem(c, SIDE)
        x_grad[0, x, y // 2, lax.rem(y, 2)] = grad[:64]
        x_grad[1, y, x // 2, lax.rem(x, 2)] = grad[64:]
        return 0

    lax.fori_loop(0, CTX, product, 0)
    first_x = plane_start(x_grad, x_ring)

    @pl.when(section == 1)
    def _():
        def one(j, _):
            columns = pl.ds(pl.multiple_of(j * TILE, TILE), TILE)
            in_out[:, columns] = (
                dsig_ref[:, columns]
                + lax.dot_general(
                    proj[:, : R + 2 * N], xw_ref[columns, :], (((1,), (1,)), ((), ())),
                    preferred_element_type=F32,
                )
            ).astype(BF16)
            return 0

        lax.fori_loop(0, u_ref.shape[1] // TILE, one, 0)
        in_copy.start()
        hin_ref[...] = jnp.zeros_like(hin_ref)
        hgate_ref[...] = jnp.zeros_like(hgate_ref)

    turned = plane_turn(step_grad, step_ring, first, lambda v, h: v[:, h * 1024 : (h + 1) * 1024])
    first_x = plane_middle(x_grad, x_ring, first_x)
    turned = plane_second_middle(step_ring, turned)
    for copy in small_home:
        copy.wait_recv()
    for c in range(CTX):
        small_ref[:, lanes(c)] = small_all[c]
    for q, halves in enumerate(plane_finish(step_ring, turned)):
        for h in range(2):
            gstep_ref[q * 16 : (q + 1) * 16, h * 1024 : (h + 1) * 1024] = halves[h]
    turned_x = plane_turn(x_grad, x_ring, first_x, lambda v, h: v[h * 32 : (h + 1) * 32])

    @pl.when(section == 0)
    def _():
        gate_copy.wait_recv()
        in_copy.wait_recv()
        hgate_ref[...] = gate_land[...]
        hin_ref[...] = in_land[...]

    turned_x = plane_second_middle(x_ring, turned_x)
    for q, halves in enumerate(plane_finish(x_ring, turned_x)):
        for h in range(2):
            gx_ref[q * 64 + h * 32 : q * 64 + (h + 1) * 32, :] = halves[h]

    @pl.when(section == 1)
    def _():
        gate_copy.wait_send()
        in_copy.wait_send()

    for copy in sums + shares + small_there + small_home:
        copy.wait_send()
    for copies in first + turned + first_x + turned_x:
        ring_done(copies)


def run_tail(part, small, dgate, step_grad, u, xw, dsig):
    ch = u.shape[1]
    f = lambda *s: jax.ShapeDtypeStruct(s, F32)
    b = lambda *s: jax.ShapeDtypeStruct(s, BF16)
    return pl.pallas_call(
        tail,
        in_specs=in_vmem(7),
        out_specs=in_vmem(5),
        out_shape=[b(TOK, ch), b(TOK, ch), f(LANE, R + 2 * N), f(32, ch), f(SMALL, ch)],
        scratch_shapes=SUM_SCRATCH
        + [pltpu.VMEM((CTX, SMALL, LANE), F32)] * 3
        + [pltpu.SemaphoreType.DMA((CTX - 1,))] * 4
        + [pltpu.VMEM((TOK, ch), BF16)] * 3
        + [pltpu.SemaphoreType.DMA((2,))] * 2
        + [pltpu.VMEM((TOK, WIDE), BF16), pltpu.VMEM((2, SIDE, 2, 2, 64, R + 2 * N), BF16)]
        + ring_scratch(STEP_UNIT, STEP_SECOND)
        + ring_scratch(X_UNIT, X_SECOND),
        compiler_params=pltpu.CompilerParams(
            collective_id=2, has_side_effects=True, vmem_limit_bytes=VMEM_BYTES
        ),
        name="tail",
    )(part, small, dgate, step_grad, u, xw, dsig)


def body(mixer_input, gate_input, upstream_grad, x_weight, step_weight, step_bias, decay_log, skip_gain):
    u, z, g = mixer_input[0], gate_input[0], upstream_grad[0]
    weight_x, weight_step = x_weight[0], step_weight[0]
    dlog = decay_log[0]
    part = jnp.dot(u, weight_x, preferred_element_type=F32)
    low, io = run_sum(jnp.pad(part, ((0, 0), (0, LANE - 2 * N))))
    step, sig, entry, leave, pack, bsum = run_first(low, io, weight_step, step_bias, dlog, u, z, g)
    across = run_exchange(pack, dlog)
    d_gate, d_signal, d_part, grad_step, small = run_second(
        low, io, weight_step, dlog, skip_gain, u, z, g, step, sig, entry, leave, bsum, across
    )
    handed_input, handed_gate, grad_x, grad_step, small = run_tail(
        d_part, small, d_gate, grad_step, u, weight_x, d_signal
    )
    return (
        handed_input[None], handed_gate[None], grad_x[None], grad_step[None],
        small[N : N + 1], small[None, :N], small[N + 1 : N + 2],
    )


def solution(mesh):
    return jax.shard_map(
        body,
        mesh=mesh,
        in_specs=(
            P("section", "ctx", "ch"), P("section", "ctx", "ch"), P("section", "ctx", "ch"),
            P("section", "ch", None), P("section", None, "ch"), P("section", "ch"),
            P("section", None, "ch"), P("section", "ch"),
        ),
        out_specs=(
            P("section", "ctx", "ch"), P("section", "ctx", "ch"), P("section", ("ch", "ctx"), None),
            P("section", "ctx", "ch"), P("section", "ch"), P("section", None, "ch"), P("section", "ch"),
        ),
        check_vma=False,
    )
```

time: 921 us -> 183 us (0.20)
  other arithmetic: 286 us -> 0 us
  waiting for transfers between devices: 280 us -> 0 us
  local copies, waits for them, and re-layouts: 203 us -> 12.1 us
  Pallas kernels: 0 us -> 167 us
  blocking collectives: 106 us -> 0 us
  matrix products: 19.5 us -> 2.89 us
  between operations: 14.4 us -> 0.71 us
    pallas_call x0 -> x5, Pallas kernels: none -> 167 us  [the longest x1 55.1 us: run_tail(): pl.pallas_call(tail, in_specs=in_vmem(7), out_specs=in_vmem(5), out_shape...]
    mul x161 -> x0, local copies, waits for them, and re-layouts: 138 us -> none  [the longest x32 27.1 us: backward_step(): adjoint = out_row[:, :, None] * seed_row[:, None, :] + incoming]
    reduce_scatter x2 -> x0, waiting for transfers between devices: 137 us -> none  [the longest x1 87.4 us: body(): lax.psum_scatter(grad_x, 'ctx', scatter_dimension=0, tiled=True)]
    psum x2 -> x0, blocking collectives: 106 us -> none  [the longest x1 68 us: body(): lax.psum((jnp.sum(d_pre, axis=0), rate_grad * rates, jnp.sum(seed * signa...]
    add x72 -> x0, other arithmetic: 92 us -> none  [the longest x16 46.5 us: forward_step(): jnp.exp(step_row[:, None, :] * rates[None]) * running]
    reduce_sum x18 -> x0, other arithmetic: 81.8 us -> none  [the longest x16 76.2 us: final_step(): grad_out_row = jnp.sum(seed_row[:, None, :] * current, axis=2)]
    psum x2 -> x0, waiting for transfers between devices: 72.6 us -> none  [the longest x1 72.5 us: body(): lax.psum(jnp.dot(signal_low, weight_x, preferred_element_type=jnp.float32...]
    all_gather x3 -> x0, waiting for transfers between devices: 71.1 us -> none  [carried_in(): gathered = jax.tree.map(lambda a: lax.all_gather(a, axis), part)]
  transfers between devices with their start and end apart: 9 -> 0, of which waited for: 5 -> 0; matrix products, arithmetic and copies ran while one was open for 14% -> 0% of each run, Pallas kernels for 0% -> 0%
where the time goes in v1:
time: 183 us
  Pallas kernels  167 us (91%)
  local copies, waits for them, and re-layouts  12.1 us (7%)
  matrix products  2.89 us (2%)
    pallas_call x1, Pallas kernels, run_tail(): pl.pallas_call(tail, in_specs=in_vmem(7), out_specs=in_vmem(5), out_shape...  55.1 us
    pallas_call x1, Pallas kernels, run_second(): pl.pallas_call(second_pass, grid=(ch // TILE,), in_specs=[whole(TOK, R),...  41.3 us
    pallas_call x1, Pallas kernels, run_sum(): pl.pallas_call(sum_projected, in_specs=in_vmem(1), out_specs=in_vmem(2),...  30.5 us
    pallas_call x1, Pallas kernels, run_first(): pl.pallas_call(first_pass, grid=(ch // TILE,), in_specs=[whole(TOK, R), w...  20.9 us
    pallas_call x1, Pallas kernels, run_exchange(): pl.pallas_call(exchange, in_specs=in_vmem(2), out_specs=pl.BlockSpec(memo...  19.4 us
    unnamed x11, local copies, waits for them, and re-layouts  8.15 us

profile of v1, /device:TPU:2, one launch (start us, length us, event | category | flops | bytes accessed | tf_op | source)
XLA Modules:
  0.0 182.9 jit_solution(1152916972341157283)
XLA Ops:
  0.6 2.9 %fusion = f32[192,544]{1,0:T(8,128)S(1)} fusion(bf16[1,2048,544]{1,2,0:T(8,128)(2,1)} %param.11, bf16[1,192,2048]{2,1,0:T(8,128)(2,1)} %param.8), kind=kOutput, calls=%fused_computation | convolution fusion | flops 427819008 | bytes 3432448 | tf_op jit(solution)/shard_map/dot_general | solution.py:766
  3.5 0.8 pad.4.part_ref
  4.3 30.5 %sum_projected.1 = (bf16[192,512]{1,0:T(8,128)(2,1)}, f32[192,128]{1,0:T(8,128)}) custom-call(f32[192,640]{1,0:T(8,128)} %pad.4.part_ref), custom_call_target="tpu_custom_call" | custom-call | tf_op jit(solution)/shard_map/sum_projected/pallas_call | solution.py:449
  34.8 20.9 %first_pass.1 = (f32[16,192,128]{2,1,0:T(8,128)}, f32[192,2048]{1,0:T(8,128)}, f32[16,8,2048]{2,1,0:T(8,128)}, f32[16,8,2048]{2,1,0:T(8,128)}, f32[16,40,128]{2,1,0:T(8,128)}, /*index=5*/f32[8,2048]{1,0:T(8,128)}) custom-call(bf16[192,512]{1,0:T(8,128)(2,1)} %get-tuple-element.25.low_ref, f32[192,128]{1,0:T(8,128)} %get-tuple-element.26.io_ref, ...), custom_call_target="tpu_custom_call" | custom-call | tf_op jit(solution)/shard_map/first_pass/pallas_call | solution.py:300
  55.8 19.4 %exchange.1.across_ref = f32[16,32,128]{2,1,0:T(8,128)} custom-call(f32[16,40,128]{2,1,0:T(8,128)} %get-tuple-element.32.pack_ref, f32[16,2048]{1,0:T(8,128)} %bitcast.28), custom_call_target="tpu_custom_call" | custom-call | tf_op jit(solution)/shard_map/exchange/pallas_call | solution.py:496
  75.2 0.0 copy-start
  75.2 41.3 %second_pass.1 = (bf16[192,2048]{1,0:T(8,128)(2,1)}, f32[192,2048]{1,0:T(8,128)}, f32[192,640]{1,0:T(8,128)}, bf16[2,4,2,2,16,2048]{5,4,3,2,1,0:T(8,128)(2,1)}, f32[16,24,128]{2,1,0:T(8,128)}) custom-call(bf16[192,512]{1,0:T(8,128)(2,1)} %get-tuple-element.25.low_ref, f32[192,128]{1,0:T(8,128)} %get-tuple-element.26.io_ref, bf16[512,2048]{1,0:T(8,128)(2,1)} %bitcast.22, ...), custom_call_target="tpu_custom_call" | custom-call | tf_op jit(solution)/shard_map/second_pass/pallas_call | solution.py:328
  116.5 0.0 copy-done
  116.5 2.6 %copy.15 = bf16[1,2048,544]{2,1,0:T(8,128)(2,1)} copy(bf16[1,2048,544]{1,2,0:T(8,128)(2,1)S(1)} %copy-done) | data formatting | bytes 4456448 | tf_op args[3]
  119.1 55.1 %tail.1 = (bf16[192,2048]{1,0:T(8,128)(2,1)}, bf16[192,2048]{1,0:T(8,128)(2,1)}, f32[128,544]{1,0:T(8,128)}, f32[32,2048]{1,0:T(8,128)}, f32[24,2048]{1,0:T(8,128)}) custom-call(f32[192,640]{1,0:T(8,128)} %get-tuple-element.33.part_ref, f32[16,24,128]{2,1,0:T(8,128)} %get-tuple-element.34.small_in, bf16[192,2048]{1,0:T(8,128)(2,1)} %get-tuple-element.35.dgate_ref, ...), custom_call_target="tpu_custom_call" | custom-call | tf_op jit(solution)/shard_map/tail/pallas_call | solution.py:742
  174.2 0.0 copy-start.1
  174.2 0.0 copy-start.2
  174.2 1.9 %copy.16 = f32[1,128,544]{1,2,0:T(8,128)} copy(f32[1,128,544]{2,1,0:T(8,128)} %bitcast.32) | data formatting | bytes 557056
  176.1 1.6 slice_bitcast_fusion
  177.7 1.5 fusion.3
  179.2 2.1 %copy.20 = bf16[1,192,2048]{2,1,0:T(8,128)(2,1)} copy(bf16[1,192,2048]{2,1,0:T(8,128)(2,1)} %bitcast.31) | data formatting | bytes 1572864
  181.3 0.0 copy-done.1
  181.3 0.9 copy.21
  182.2 0.0 copy-done.2
  182.2 0.7 copy.22
Async XLA Ops:
  75.2 41.3 %copy-start = (bf16[1,2048,544]{1,2,0:T(8,128)(2,1)S(1)}, bf16[1,2048,544]{1,2,0:T(8,128)(2,1)}, u32[]{:S(2)}) copy-start(bf16[1,2048,544]{1,2,0:T(8,128)(2,1)} %param.11) | copy-start | bytes 6684676
  174.2 7.1 %copy-start.1 = (bf16[192,2048]{1,0:T(8,128)(2,1)S(1)}, bf16[192,2048]{1,0:T(8,128)(2,1)}, u32[]{:S(2)}) copy-start(bf16[192,2048]{1,0:T(8,128)(2,1)} %get-tuple-element.39) | copy-start | bytes 2359300
  174.2 8.0 %copy-start.2 = (f32[32,2048]{1,0:T(8,128)S(1)}, f32[32,2048]{1,0:T(8,128)}, u32[]{:S(2)}) copy-start(f32[32,2048]{1,0:T(8,128)} %get-tuple-element.41) | copy-start | bytes 786436

commit v2 on v1

--- a/solution.py
+++ b/solution.py
@@ -39,13 +39,18 @@
     return slice(k * LANE, (k + 1) * LANE)
 
 
-def by_lanes(ref, value):
+def by_step(ref, value, by_token):
     for k in range(HALVES):
-        ref[k] = value[:, lanes(k)]
-
-
-def joined(ref):
-    return jnp.concatenate([ref[k] for k in range(HALVES)], axis=1)
+        by_token[k] = value[:, lanes(k)]
+        for i in range(STEPS):
+            ref[k, i] = by_token[k, every(i), :]
+
+
+def from_step(ref, by_token):
+    for k in range(HALVES):
+        for i in range(STEPS):
+            by_token[k, every(i), :] = ref[k, i]
+    return jnp.concatenate([by_token[k] for k in range(HALVES)], axis=1)
 
 
 def row_index():
@@ -75,8 +80,8 @@
 
 def first_pass(
     low_ref, io_ref, w_ref, bias_ref, dlog_ref, u_ref, z_ref, g_ref,
-    step_ref, sig_ref, entry_ref, exit_ref, pack_ref, bsum_ref,
-    spread, drive, seed, rates,
+    step_ref, token_ref, sig_ref, drive, seed, entry_ref, exit_ref, pack_ref, bsum_ref,
+    spread, by_drive, by_seed, by_step_size, rates,
 ):
     @pl.when(pl.program_id(0) == 0)
     def _():
@@ -86,15 +91,16 @@
     step = jnp.maximum(pre, 0.0) + jnp.log1p(jnp.exp(-jnp.abs(pre)))
     sig_ref[...] = jax.nn.sigmoid(pre)
     z = z_ref[...].astype(F32)
-    by_lanes(step_ref, step)
-    by_lanes(drive, step * u_ref[...].astype(F32))
-    by_lanes(seed, g_ref[...].astype(F32) * z * jax.nn.sigmoid(z))
+    token_ref[...] = step
+    by_step(step_ref, step, by_step_size)
+    by_step(drive, step * u_ref[...].astype(F32), by_drive)
+    by_step(seed, g_ref[...].astype(F32) * z * jax.nn.sigmoid(z), by_seed)
     rates[...] = -LOG2E * jnp.exp(dlog_ref[...])
     row = row_index()
 
     total = jnp.zeros((ROWS, TILE), F32)
     for i in range(STEPS):
-        total = total + jnp.concatenate([step_ref[k, every(i), :] for k in range(HALVES)], axis=1)
+        total = total + jnp.concatenate([step_ref[k, i] for k in range(HALVES)], axis=1)
     bsum_ref[...] = total
     whole_sum = jnp.sum(total, axis=0, keepdims=True)
     for k in range(HALVES):
@@ -106,9 +112,9 @@
 
         def one(i, carry):
             state, decay, start = carry
-            st = [step_ref[k, every(i), :] for k in range(HALVES)]
-            dr = [drive[k, every(i), :] for k in range(HALVES)]
-            sd = [seed[k, every(i), :] for k in range(HALVES)]
+            st = [step_ref[k, i] for k in range(HALVES)]
+            dr = [drive[k, i] for k in range(HALVES)]
+            sd = [seed[k, i] for k in range(HALVES)]
             new_state, new_decay, new_start = [], [], []
             for p, (n, k) in enumerate(pairs):
                 a = jnp.exp2(st[k] * rate[p])
@@ -141,10 +147,10 @@
 
 
 def second_pass(
-    low_ref, io_ref, w_ref, dlog_ref, skip_ref, u_ref, z_ref, g_ref, step_ref, sig_ref,
+    low_ref, io_ref, w_ref, dlog_ref, skip_ref, u_ref, z_ref, g_ref, step_ref, token_ref, sig_ref, drive, seed,
     entry_ref, exit_ref, bsum_ref, across_ref,
     dgate_ref, dsig_ref, part_ref, gstep_ref, small_ref,
-    spread, sums, held, drive, seed, scanned, grad_drive, grad_decay, rates, by_token,
+    spread, sums, held, scanned, grad_drive, grad_decay, by_scan, by_grad, by_decay, rates, by_token,
 ):
     tile = pl.program_id(0)
 
@@ -154,13 +160,6 @@
         sums[...] = jnp.zeros_like(sums)
         part_ref[...] = jnp.zeros_like(part_ref)
 
-    step = joined(step_ref)
-    u = u_ref[...].astype(F32)
-    z = z_ref[...].astype(F32)
-    g = g_ref[...].astype(F32)
-    gate_sig = jax.nn.sigmoid(z)
-    by_lanes(drive, step * u)
-    by_lanes(seed, g * z * gate_sig)
     rates[...] = -LOG2E * jnp.exp(dlog_ref[...])
     scanned[...] = jnp.zeros_like(scanned)
     grad_drive[...] = jnp.zeros_like(grad_drive)
@@ -174,10 +173,10 @@
         rate = [jnp.broadcast_to(rates[n : n + 1, lanes(k)], (ROWS, LANE)) for n, k in pairs]
 
         def forward(i, state):
-            st = [step_ref[k, every(i), :] for k in range(HALVES)]
-            dr = [drive[k, every(i), :] for k in range(HALVES)]
-            sd = [seed[k, every(i), :] for k in range(HALVES)]
-            out = [scanned[k, every(i), :] for k in range(HALVES)]
+            st = [step_ref[k, i] for k in range(HALVES)]
+            dr = [drive[k, i] for k in range(HALVES)]
+            sd = [seed[k, i] for k in range(HALVES)]
+            out = [scanned[k, i] for k in range(HALVES)]
             new = []
             for m, n in enumerate(numbers):
                 b_in, b_out = spread[i, n], spread[i, N + n]
@@ -191,7 +190,7 @@
                     d_out = d_out + sd[k] * now
                 sums[i, N + n] = d_out
             for k in range(HALVES):
-                scanned[k, every(i), :] = out[k]
+                scanned[k, i] = out[k]
             return tuple(new)
 
         state = tuple(
@@ -204,11 +203,11 @@
         def backward(j, carry):
             incoming, total = carry
             i = STEPS - 1 - j
-            st = [step_ref[k, every(i), :] for k in range(HALVES)]
-            dr = [drive[k, every(i), :] for k in range(HALVES)]
-            sd = [seed[k, every(i), :] for k in range(HALVES)]
-            g_drive = [grad_drive[k, every(i), :] for k in range(HALVES)]
-            g_decay = [grad_decay[k, every(i), :] for k in range(HALVES)]
+            st = [step_ref[k, i] for k in range(HALVES)]
+            dr = [drive[k, i] for k in range(HALVES)]
+            sd = [seed[k, i] for k in range(HALVES)]
+            g_drive = [grad_drive[k, i] for k in range(HALVES)]
+            g_decay = [grad_decay[k, i] for k in range(HALVES)]
             new_in, new_total = [], []
             for m, n in enumerate(numbers):
                 b_in, b_out = spread[i, n], spread[i, N + n]
@@ -225,8 +224,8 @@
                     d_in = d_in + adjoint * dr[k]
                 sums[i, n] = d_in
             for k in range(HALVES):
-                grad_drive[k, every(i), :] = g_drive[k]
-                grad_decay[k, every(i), :] = g_decay[k]
+                grad_drive[k, i] = g_drive[k]
+                grad_decay[k, i] = g_decay[k]
             return tuple(new_in), tuple(new_total)
 
         incoming = tuple(
@@ -241,13 +240,17 @@
                 jnp.sum(total[p], axis=0, keepdims=True) * rates[n : n + 1, lanes(k)] * LN2
             )
 
+    u = u_ref[...].astype(F32)
+    z = z_ref[...].astype(F32)
+    g = g_ref[...].astype(F32)
+    gate_sig = jax.nn.sigmoid(z)
+    seeds = g * z * gate_sig
     skip = skip_ref[...]
-    by_drive = joined(grad_drive)
-    seeds = joined(seed)
-    mixed = joined(scanned) + skip * u
+    from_drive = from_step(grad_drive, by_grad)
+    mixed = from_step(scanned, by_scan) + skip * u
     dgate_ref[...] = (g * mixed * gate_sig * (1.0 + z * (1.0 - gate_sig))).astype(BF16)
-    dsig_ref[...] = by_drive * step + skip * seeds
-    d_pre = (by_drive * u + joined(grad_decay) * LN2) * sig_ref[...]
+    dsig_ref[...] = from_drive * token_ref[...] + skip * seeds
+    d_pre = (from_drive * u + from_step(grad_decay, by_decay) * LN2) * sig_ref[...]
     pre = d_pre.astype(BF16)
     bias_row = jnp.sum(d_pre, axis=0, keepdims=True)
     skip_row = jnp.sum(seeds * u, axis=0, keepdims=True)
@@ -290,8 +293,8 @@
     return pl.BlockSpec(lead + (TILE,), lambda j: (0,) * len(lead) + (j,))
 
 
-def stacked(rows):
-    return pl.BlockSpec((HALVES, rows, LANE), lambda j: (j, 0, 0))
+def stacked(*rows):
+    return pl.BlockSpec((HALVES,) + rows + (LANE,), lambda j: (j,) + (0,) * (len(rows) + 1))
 
 
 def run_first(low, io, weight, bias, dlog, u, z, g):
@@ -305,14 +308,17 @@
             tiled(TOK), tiled(TOK), tiled(TOK),
         ],
         out_specs=[
-            stacked(TOK), tiled(TOK), tiled(N, ROWS), tiled(N, ROWS), stacked(PACK), tiled(ROWS),
+            stacked(STEPS, ROWS), tiled(TOK), tiled(TOK), stacked(STEPS, ROWS), stacked(STEPS, ROWS),
+            tiled(N, ROWS), tiled(N, ROWS), stacked(PACK), tiled(ROWS),
         ],
         out_shape=[
-            f(ch // LANE, TOK, LANE), f(TOK, ch), f(N, ROWS, ch), f(N, ROWS, ch),
+            f(ch // LANE, STEPS, ROWS, LANE), f(TOK, ch), f(TOK, ch), f(ch // LANE, STEPS, ROWS, LANE),
+            f(ch // LANE, STEPS, ROWS, LANE), f(N, ROWS, ch), f(N, ROWS, ch),
             f(ch // LANE, PACK, LANE), f(ROWS, ch),
         ],
         scratch_shapes=[
             pltpu.VMEM((STEPS, 2 * N, ROWS, LANE), F32),
+            pltpu.VMEM((HALVES, TOK, LANE), F32),
             pltpu.VMEM((HALVES, TOK, LANE), F32),
             pltpu.VMEM((HALVES, TOK, LANE), F32),
             pltpu.VMEM((N, TILE), F32),
@@ -322,7 +328,7 @@
     )(low, io, weight, bias, dlog, u, z, g)
 
 
-def run_second(low, io, weight, dlog, skip, u, z, g, step, sig, entry, leave, bsum, across):
+def run_second(low, io, weight, dlog, skip, u, z, g, kept, across):
     ch = u.shape[1]
     f = lambda *s: jax.ShapeDtypeStruct(s, F32)
     return pl.pallas_call(
@@ -330,8 +336,8 @@
         grid=(ch // TILE,),
         in_specs=[
             whole(TOK, R), whole(TOK, io.shape[1]), tiled(R), tiled(N), tiled(1),
-            tiled(TOK), tiled(TOK), tiled(TOK), stacked(TOK), tiled(TOK),
-            tiled(N, ROWS), tiled(N, ROWS), tiled(ROWS), stacked(2 * N),
+            tiled(TOK), tiled(TOK), tiled(TOK), stacked(STEPS, ROWS), tiled(TOK), tiled(TOK),
+            stacked(STEPS, ROWS), stacked(STEPS, ROWS), tiled(N, ROWS), tiled(N, ROWS), tiled(ROWS), stacked(2 * N),
         ],
         out_specs=[
             tiled(TOK), tiled(TOK), whole(TOK, WIDE), tiled(2, SIDE, 2, 2, 16), stacked(SMALL),
@@ -345,11 +351,12 @@
             pltpu.VMEM((STEPS, 2 * N, ROWS, LANE), F32),
             pltpu.VMEM((STEPS, CHUNK, ROWS, TILE), F32),
         ]
-        + [pltpu.VMEM((HALVES, TOK, LANE), F32)] * 5
+        + [pltpu.VMEM((HALVES, STEPS, ROWS, LANE), F32)] * 3
+        + [pltpu.VMEM((HALVES, TOK, LANE), F32)] * 3
         + [pltpu.VMEM((N, TILE), F32), pltpu.VMEM((TOK, LANE), F32)],
         compiler_params=pltpu.CompilerParams(vmem_limit_bytes=VMEM_BYTES),
         name="second_pass",
-    )(low, io, weight, dlog, skip, u, z, g, step, sig, entry, leave, bsum, across)
+    )(low, io, weight, dlog, skip, u, z, g, *kept, across)
 
 
 def greet(partners):
@@ -374,28 +381,45 @@
     return pl.ds(pl.multiple_of(owner * PIECE, 8), PIECE)
 
 
-def sum_start(part_ref, landed, send, recv):
+def fold(rows):
+    return rows[:ROWS] + pltpu.roll(rows[ROWS : 2 * ROWS], 2 * N, 1) + pltpu.roll(rows[2 * ROWS :], 4 * N, 1)
+
+
+def unfold(folded):
+    used = lax.broadcasted_iota(jnp.int32, (ROWS, LANE), 1) < 2 * N
+    parts = [folded, pltpu.roll(folded, LANE - 2 * N, 1), pltpu.roll(folded, LANE - 4 * N, 1)]
+    return jnp.concatenate([jnp.where(used, part, 0.0) for part in parts], axis=0)
+
+
+def over(rows):
+    return jnp.concatenate([rows[:, : R // 2], rows[:, R // 2 : R]], axis=0)
+
+
+def sum_start(part_ref, low_part, io_part, low_land, io_land, send, recv):
+    for p in range(CH):
+        rows = part_ref[p * PIECE : (p + 1) * PIECE, :]
+        low_part[p] = over(rows).astype(low_part.dtype)
+        io_part[p] = fold(rows[:, R:])
     copies = []
     for d, to in enumerate(others("ch", CH)):
-        copies.append(remote(part_ref.at[token_rows(to["ch"])], landed.at[d], send.at[d], recv.at[d], to))
-        copies[-1].start()
+        copies.append(remote(low_part.at[to["ch"]], low_land.at[d], send.at[0, d], recv.at[0, d], to))
+        copies.append(remote(io_part.at[to["ch"]], io_land.at[d], send.at[1, d], recv.at[1, d], to))
+    for copy in copies:
+        copy.start()
     return copies
 
 
-def sum_finish(copies, part_ref, landed):
+def share_start(sums, part_ref, io_part, low_land, io_land, low_all, io_all, send, recv):
     me = lax.axis_index("ch")
-    for copy in copies:
+    for copy in sums:
         copy.wait_recv()
-    total = part_ref[token_rows(me), :]
+    low = over(part_ref[token_rows(me), :])
+    io = io_part[me]
     for d in range(CH - 1):
-        total = total + landed[d]
-    return total
-
-
-def share_start(total, low_all, io_all, send, recv):
-    me = lax.axis_index("ch")
-    low_all[me] = jnp.concatenate([total[:, : R // 2], total[:, R // 2 : R]], axis=0).astype(BF16)
-    io_all[me] = total[:, R:]
+        low = low + low_land[d].astype(F32)
+        io = io + io_land[d]
+    low_all[me] = low.astype(BF16)
+    io_all[me] = io
     copies = []
     for d, to in enumerate(others("ch", CH)):
         copies.append(remote(low_all.at[me], low_all.at[me], send.at[0, d], recv.at[0, d], to))
@@ -413,27 +437,34 @@
         rows = slice(p * PIECE, (p + 1) * PIECE)
         wide[rows, : R // 2] = both[:PIECE]
         wide[rows, R // 2 : R] = both[PIECE:]
-        wide[rows, R:] = io_all[p]
-
-
-SUM_SCRATCH = [
-    pltpu.VMEM((CH - 1, PIECE, WIDE), F32),
-    pltpu.VMEM((CH, 2 * PIECE, R // 2), BF16),
-    pltpu.VMEM((CH, PIECE, LANE), F32),
-    pltpu.VMEM((TOK, WIDE), F32),
-    pltpu.SemaphoreType.DMA((CH - 1,)),
-    pltpu.SemaphoreType.DMA((CH - 1,)),
-    pltpu.SemaphoreType.DMA((2, CH - 1)),
-    pltpu.SemaphoreType.DMA((2, CH - 1)),
-]
-
-
-def sum_projected(
-    part_ref, low_ref, io_ref, landed, low_all, io_all, wide, sum_send, sum_recv, all_send, all_recv
-):
+        wide[rows, R:] = unfold(io_all[p])
+
+
+def sum_scratch(sent):
+    return [
+        pltpu.VMEM((CH, 2 * PIECE, R // 2), sent),
+        pltpu.VMEM((CH, ROWS, LANE), F32),
+        pltpu.VMEM((CH - 1, 2 * PIECE, R // 2), sent),
+        pltpu.VMEM((CH - 1, ROWS, LANE), F32),
+        pltpu.VMEM((CH, 2 * PIECE, R // 2), BF16),
+        pltpu.VMEM((CH, ROWS, LANE), F32),
+        pltpu.VMEM((TOK, WIDE), F32),
+        pltpu.SemaphoreType.DMA((2, CH - 1)),
+        pltpu.SemaphoreType.DMA((2, CH - 1)),
+        pltpu.SemaphoreType.DMA((2, CH - 1)),
+        pltpu.SemaphoreType.DMA((2, CH - 1)),
+    ]
+
+
+def sum_projected(u_ref, xt_ref, low_ref, io_ref, part_ref, *scratch):
+    low_part, io_part, low_land, io_land, low_all, io_all, wide, sum_send, sum_recv, all_send, all_recv = scratch
+    part_ref[:, R:] = jnp.zeros((TOK, LANE), F32)
+    part_ref[:, : R + 2 * N] = lax.dot_general(
+        u_ref[...], xt_ref[...], (((1,), (1,)), ((), ())), preferred_element_type=F32
+    )
     greet(others("ch", CH))
-    sums = sum_start(part_ref, landed, sum_send, sum_recv)
-    shares = share_start(sum_finish(sums, part_ref, landed), low_all, io_all, all_send, all_recv)
+    sums = sum_start(part_ref, low_part, io_part, low_land, io_land, sum_send, sum_recv)
+    shares = share_start(sums, part_ref, io_part, low_land, io_land, low_all, io_all, all_send, all_recv)
     share_finish(shares, low_all, io_all, wide)
     low_ref[...] = wide[:, :R].astype(BF16)
     io_ref[...] = wide[:, R:]
@@ -445,18 +476,18 @@
     return [pl.BlockSpec(memory_space=pltpu.VMEM)] * count
 
 
-def run_sum(part):
+def run_sum(u, xt):
     return pl.pallas_call(
         sum_projected,
-        in_specs=in_vmem(1),
+        in_specs=in_vmem(2),
         out_specs=in_vmem(2),
         out_shape=[jax.ShapeDtypeStruct((TOK, R), BF16), jax.ShapeDtypeStruct((TOK, LANE), F32)],
-        scratch_shapes=SUM_SCRATCH,
+        scratch_shapes=[pltpu.VMEM((TOK, WIDE), F32)] + sum_scratch(F32),
         compiler_params=pltpu.CompilerParams(
             collective_id=0, has_side_effects=True, vmem_limit_bytes=VMEM_BYTES
         ),
         name="sum_projected",
-    )(part)
+    )(u, xt)
 
 
 def spread_start(src, dst, send, recv):
@@ -572,80 +603,90 @@
             copy.wait_send()
 
 
+RING = 9
+
+
 def ring_scratch(unit, second):
     return [
+        pltpu.VMEM((2,) + unit, BF16),
         pltpu.VMEM((2, 2) + unit, BF16),
-        pltpu.VMEM((2, 2, 2) + unit, BF16),
-        pltpu.VMEM((2, SIDE, 2) + second, BF16),
+        pltpu.VMEM((SIDE, 2) + second, BF16),
+        pltpu.VMEM((2,) + second, BF16),
         pltpu.VMEM((2, 2) + second, BF16),
-        pltpu.VMEM((2, 2, 2) + second, BF16),
-        pltpu.SemaphoreType.DMA((2, 3, 2)),
-        pltpu.SemaphoreType.DMA((2, 3, 2)),
-        pltpu.SemaphoreType.DMA((2, 3, 2)),
-        pltpu.SemaphoreType.DMA((2, 3, 2)),
+        pltpu.SemaphoreType.DMA((3, 2)),
+        pltpu.SemaphoreType.DMA((3, 2)),
+        pltpu.SemaphoreType.DMA((3, 2)),
+        pltpu.SemaphoreType.DMA((3, 2)),
     ]
 
 
-STEP_UNIT, STEP_SECOND = (2, 16, 2048), (16, 1024)
-X_UNIT, X_SECOND = (2, 64, R + 2 * N), (32, R + 2 * N)
-
-
-def plane_start(src, scratch):
-    relay, land, _, _, _, send, recv, _, _ = scratch
-    return [
-        ring_start(q, src.at[q], relay.at[q], land.at[q], send.at[q], recv.at[q]) for q in range(2)
-    ]
-
-
-def plane_middle(src, scratch, copies):
-    relay, land, _, _, _, send, recv, _, _ = scratch
-    return [
-        ring_middle(q, src.at[q], relay.at[q], land.at[q], send.at[q], recv.at[q], copies[q]) for q in range(2)
-    ]
-
-
-def plane_turn(src, scratch, copies, split):
-    _, land, second, relay, land2, _, _, send, recv = scratch
+def plane_start(src, rings):
     started = []
-    for q in range(2):
-        halves = ring_finish(q, src.at[q], land.at[q], copies[q])
+    for q, (relay, land, _, _, _, send, recv, _, _) in enumerate(rings):
+        started.append(ring_start(q, src[q], relay, land, send, recv))
+    return started
+
+
+def plane_middle(src, rings, copies):
+    passed = []
+    for q, (relay, land, _, _, _, send, recv, _, _) in enumerate(rings):
+        passed.append(ring_middle(q, src[q], relay, land, send, recv, copies[q]))
+    return passed
+
+
+def plane_turn(src, rings, copies, split):
+    started = []
+    for q, (_, land, second, relay, land2, _, _, send, recv) in enumerate(rings):
+        halves = ring_finish(q, src[q], land, copies[q])
         for o in range(SIDE):
             for h in range(2):
-                second[q, o, h] = split(halves[o // 2][o % 2], h).astype(BF16)
-        started.append(
-            ring_start(1 - q, second.at[q], relay.at[q], land2.at[q], send.at[q], recv.at[q])
-        )
+                second[o, h] = split(halves[o // 2][o % 2], h).astype(BF16)
+        started.append(ring_start(1 - q, second, relay, land2, send, recv))
     return started
 
 
-def plane_second_middle(scratch, copies):
-    _, _, second, relay, land, _, _, send, recv = scratch
-    return [
-        ring_middle(1 - q, second.at[q], relay.at[q], land.at[q], send.at[q], recv.at[q], copies[q])
-        for q in range(2)
-    ]
-
-
-def plane_finish(scratch, copies):
-    second, land = scratch[2], scratch[4]
-    return [ring_finish(1 - q, second.at[q], land.at[q], copies[q]) for q in range(2)]
+def plane_second_middle(rings, copies):
+    passed = []
+    for q, (_, _, second, relay, land2, _, _, send, recv) in enumerate(rings):
+        passed.append(ring_middle(1 - q, second, relay, land2, send, recv, copies[q]))
+    return passed
+
+
+def plane_finish(rings, copies):
+    return [ring_finish(1 - q, rings[q][2], rings[q][4], copies[q]) for q in range(2)]
+
+
+def left_half(value, h):
+    columns = value.shape[1] // 2
+    return value[:, h * columns : (h + 1) * columns]
+
+
+def top_half(value, h):
+    rows = value.shape[0] // 2
+    return value[h * rows : (h + 1) * rows]
+
+
+X_ROWS = (288, 256)
 
 
 def tail(
     part_ref, small_in, dgate_ref, step_grad, u_ref, xw_ref, dsig_ref,
-    hin_ref, hgate_ref, gx_ref, gstep_ref, small_ref,
-    landed, low_all, io_all, wide, sum_send, sum_recv, all_send, all_recv,
+    hin_ref, hgate_ref, gx_ref, gstep_ref, gdecay_ref, gbias_ref, gskip_ref,
+    low_part, io_part, low_land, io_land, low_all, io_all, wide, sum_send, sum_recv, all_send, all_recv,
     small_land, small_back, small_all, s_send, s_recv, t_send, t_recv,
-    gate_land, in_out, in_land, hand_send, hand_recv, proj, x_grad, *rings,
+    gate_land, in_out, in_land, hand_send, hand_recv, proj, proj_t, x_grad0, x_grad1, *scratch,
 ):
-    step_ring, x_ring = rings[:9], rings[9:]
+    rings = [scratch[k * RING : (k + 1) * RING] for k in range(4)]
+    step_ring, x_ring = rings[:2], rings[2:]
+    step_grad = [step_grad.at[q] for q in range(2)]
+    x_grad = [x_grad0, x_grad1]
     section = lax.axis_index("section")
     me = lax.axis_index("ctx")
     greet(others("ctx", CTX) + others("ch", CH) + [{"section": 1 - section}])
     gate_copy = remote(dgate_ref, gate_land, hand_send.at[0], hand_recv.at[0], {"section": 1 - section})
     in_copy = remote(in_out, in_land, hand_send.at[1], hand_recv.at[1], {"section": 1 - section})
 
-    sums = sum_start(part_ref, landed, sum_send, sum_recv)
+    sums = sum_start(part_ref, low_part, io_part, low_land, io_land, sum_send, sum_recv)
     first = plane_start(step_grad, step_ring)
 
     @pl.when(section == 1)
@@ -653,7 +694,7 @@
         gate_copy.start()
 
     small_there = spread_start(small_in, small_land, s_send, s_recv)
-    shares = share_start(sum_finish(sums, part_ref, landed), low_all, io_all, all_send, all_recv)
+    shares = share_start(sums, part_ref, io_part, low_land, io_land, low_all, io_all, all_send, all_recv)
     first = plane_middle(step_grad, step_ring, first)
     for copy in small_there:
         copy.wait_recv()
@@ -668,18 +709,20 @@
 
     share_finish(shares, low_all, io_all, wide)
     proj[...] = wide[...].astype(BF16)
+    proj_t[...] = wide[...].T.astype(BF16)
 
     def product(c, _):
-        columns = pl.ds(pl.multiple_of(c * LANE, LANE), LANE)
-        grad = lax.dot_general(
-            u_ref[:, columns], proj[...], (((0,), (0,)), ((), ())), preferred_element_type=F32
-        )[:, : R + 2 * N].astype(BF16)
-        x, y = c // SIDE, lax.rem(c, SIDE)
-        x_grad[0, x, y // 2, lax.rem(y, 2)] = grad[:64]
-        x_grad[1, y, x // 2, lax.rem(x, 2)] = grad[64:]
+        columns = pl.ds(pl.multiple_of(c * TILE, TILE), TILE)
+        grad = jnp.dot(
+            proj_t[: R + 2 * N, :], u_ref[:, columns], preferred_element_type=F32
+        ).astype(BF16)
+        x, y_high = c // 2, lax.rem(c, 2)
+        for e in range(2):
+            x_grad0[x, y_high, e] = grad[: X_ROWS[0], lanes(e)]
+            x_grad1[2 * y_high + e, x // 2, lax.rem(x, 2)] = grad[X_ROWS[0] :, lanes(e)]
         return 0
 
-    lax.fori_loop(0, CTX, product, 0)
+    lax.fori_loop(0, CTX // 2, product, 0)
     first_x = plane_start(x_grad, x_ring)
 
     @pl.when(section == 1)
@@ -689,7 +732,7 @@
             in_out[:, columns] = (
                 dsig_ref[:, columns]
                 + lax.dot_general(
-                    proj[:, : R + 2 * N], xw_ref[columns, :], (((1,), (1,)), ((), ())),
+                    proj[:, : R + 2 * N], xw_ref[:, columns], (((1,), (0,)), ((), ())),
                     preferred_element_type=F32,
                 )
             ).astype(BF16)
@@ -700,17 +743,19 @@
         hin_ref[...] = jnp.zeros_like(hin_ref)
         hgate_ref[...] = jnp.zeros_like(hgate_ref)
 
-    turned = plane_turn(step_grad, step_ring, first, lambda v, h: v[:, h * 1024 : (h + 1) * 1024])
+    turned = plane_turn(step_grad, step_ring, first, left_half)
     first_x = plane_middle(x_grad, x_ring, first_x)
     turned = plane_second_middle(step_ring, turned)
     for copy in small_home:
         copy.wait_recv()
     for c in range(CTX):
-        small_ref[:, lanes(c)] = small_all[c]
+        gdecay_ref[:, lanes(c)] = small_all[c, :N]
+        gbias_ref[:, lanes(c)] = small_all[c, N : N + 1]
+        gskip_ref[:, lanes(c)] = small_all[c, N + 1 : N + 2]
     for q, halves in enumerate(plane_finish(step_ring, turned)):
         for h in range(2):
             gstep_ref[q * 16 : (q + 1) * 16, h * 1024 : (h + 1) * 1024] = halves[h]
-    turned_x = plane_turn(x_grad, x_ring, first_x, lambda v, h: v[h * 32 : (h + 1) * 32])
+    turned_x = plane_turn(x_grad, x_ring, first_x, top_half)
 
     @pl.when(section == 0)
     def _():
@@ -722,7 +767,8 @@
     turned_x = plane_second_middle(x_ring, turned_x)
     for q, halves in enumerate(plane_finish(x_ring, turned_x)):
         for h in range(2):
-            gx_ref[q * 64 + h * 32 : q * 64 + (h + 1) * 32, :] = halves[h]
+            rows = X_ROWS[q] // 2
+            gx_ref[q * X_ROWS[0] + h * rows : q * X_ROWS[0] + (h + 1) * rows, :] = halves[h]
 
     @pl.when(section == 1)
     def _():
@@ -742,16 +788,20 @@
     return pl.pallas_call(
         tail,
         in_specs=in_vmem(7),
-        out_specs=in_vmem(5),
-        out_shape=[b(TOK, ch), b(TOK, ch), f(LANE, R + 2 * N), f(32, ch), f(SMALL, ch)],
-        scratch_shapes=SUM_SCRATCH
+        out_specs=in_vmem(7),
+        out_shape=[
+            b(TOK, ch), b(TOK, ch), f(R + 2 * N, LANE), f(32, ch), f(N, ch), f(1, ch), f(1, ch),
+        ],
+        scratch_shapes=sum_scratch(BF16)
         + [pltpu.VMEM((CTX, SMALL, LANE), F32)] * 3
         + [pltpu.SemaphoreType.DMA((CTX - 1,))] * 4
         + [pltpu.VMEM((TOK, ch), BF16)] * 3
         + [pltpu.SemaphoreType.DMA((2,))] * 2
-        + [pltpu.VMEM((TOK, WIDE), BF16), pltpu.VMEM((2, SIDE, 2, 2, 64, R + 2 * N), BF16)]
-        + ring_scratch(STEP_UNIT, STEP_SECOND)
-        + ring_scratch(X_UNIT, X_SECOND),
+        + [pltpu.VMEM((TOK, WIDE), BF16), pltpu.VMEM((WIDE, TOK), BF16)]
+        + [pltpu.VMEM((SIDE, 2, 2, rows, LANE), BF16) for rows in X_ROWS]
+        + ring_scratch((2, 16, 2048), (16, 1024)) * 2
+        + ring_scratch((2, X_ROWS[0], LANE), (X_ROWS[0] // 2, LANE))
+        + ring_scratch((2, X_ROWS[1], LANE), (X_ROWS[1] // 2, LANE)),
         compiler_params=pltpu.CompilerParams(
             collective_id=2, has_side_effects=True, vmem_limit_bytes=VMEM_BYTES
         ),
@@ -759,23 +809,45 @@
     )(part, small, dgate, step_grad, u, xw, dsig)
 
 
+def finish(*refs):
+    count = len(refs) // 2
+    sem = refs[-1]
+    copies = [pltpu.make_async_copy(refs[k], refs[count + k], sem.at[k]) for k in range(count)]
+    for copy in copies:
+        copy.start()
+    for copy in copies:
+        copy.wait()
+
+
+def run_finish(*results):
+    anywhere = [pl.BlockSpec(memory_space=pl.ANY)] * len(results)
+    return pl.pallas_call(
+        finish,
+        in_specs=anywhere,
+        out_specs=anywhere,
+        out_shape=[jax.ShapeDtypeStruct(r.shape, r.dtype) for r in results],
+        scratch_shapes=[pltpu.SemaphoreType.DMA((len(results),))],
+        compiler_params=pltpu.CompilerParams(vmem_limit_bytes=VMEM_BYTES),
+        name="finish",
+    )(*results)
+
+
 def body(mixer_input, gate_input, upstream_grad, x_weight, step_weight, step_bias, decay_log, skip_gain):
     u, z, g = mixer_input[0], gate_input[0], upstream_grad[0]
-    weight_x, weight_step = x_weight[0], step_weight[0]
+    weight_x, weight_step = jnp.swapaxes(x_weight[0], 0, 1), step_weight[0]
     dlog = decay_log[0]
-    part = jnp.dot(u, weight_x, preferred_element_type=F32)
-    low, io = run_sum(jnp.pad(part, ((0, 0), (0, LANE - 2 * N))))
-    step, sig, entry, leave, pack, bsum = run_first(low, io, weight_step, step_bias, dlog, u, z, g)
+    low, io = run_sum(u, weight_x)
+    *kept, pack, bsum = run_first(low, io, weight_step, step_bias, dlog, u, z, g)
     across = run_exchange(pack, dlog)
     d_gate, d_signal, d_part, grad_step, small = run_second(
-        low, io, weight_step, dlog, skip_gain, u, z, g, step, sig, entry, leave, bsum, across
+        low, io, weight_step, dlog, skip_gain, u, z, g, [*kept, bsum], across
     )
-    handed_input, handed_gate, grad_x, grad_step, small = run_tail(
-        d_part, small, d_gate, grad_step, u, weight_x, d_signal
+    handed_input, handed_gate, grad_x, grad_step, g_decay, g_bias, g_skip = run_finish(
+        *run_tail(d_part, small, d_gate, grad_step, u, weight_x, d_signal)
     )
     return (
-        handed_input[None], handed_gate[None], grad_x[None], grad_step[None],
-        small[N : N + 1], small[None, :N], small[N + 1 : N + 2],
+        handed_input[None], handed_gate[None], jnp.swapaxes(grad_x, 0, 1)[None], grad_step[None],
+        g_bias, g_decay[None], g_skip,
     )
 
 

time: 183 us -> 223 us (1.22)
  Pallas kernels: 167 us -> 223 us
  local copies, waits for them, and re-layouts: 12.1 us -> 0 us
  matrix products: 2.89 us -> 0 us
    pallas_call x2 -> x3, Pallas kernels: 85.6 us -> 146 us  [the longest x1 69.7 us: run_finish(): pl.pallas_call(finish, in_specs=anywhere, out_specs=anywhere, out_shape=[...]
    unnamed x11 -> x0, local copies, waits for them, and re-layouts: 8.15 us -> none
    pallas_call x1, Pallas kernels: 41.3 us -> 36.7 us  [run_second(): pl.pallas_call(second_pass, grid=(ch // TILE,), in_specs=[whole(TOK, R),...]
    dot_general x1 -> x0, matrix products: 2.89 us -> none  [body(): part = jnp.dot(u, weight_x, preferred_element_type=F32)]
where the time goes in v2:
time: 223 us
  Pallas kernels  223 us (100%)
    pallas_call x1, Pallas kernels, run_finish(): pl.pallas_call(finish, in_specs=anywhere, out_specs=anywhere, out_shape=[...  69.7 us
    pallas_call x1, Pallas kernels, run_tail(): pl.pallas_call(tail, in_specs=in_vmem(7), out_specs=in_vmem(7), out_shape...  45.6 us
    pallas_call x1, Pallas kernels, run_second(): pl.pallas_call(second_pass, grid=(ch // TILE,), in_specs=[whole(TOK, R),...  36.7 us
    pallas_call x1, Pallas kernels, run_sum(): pl.pallas_call(sum_projected, in_specs=in_vmem(2), out_specs=in_vmem(2),...  31 us
    pallas_call x1, Pallas kernels, run_first(): pl.pallas_call(first_pass, grid=(ch // TILE,), in_specs=[whole(TOK, R), w...  20.7 us
    pallas_call x1, Pallas kernels, run_exchange(): pl.pallas_call(exchange, in_specs=in_vmem(2), out_specs=pl.BlockSpec(memo...  18.8 us

profile of v2, /device:TPU:2, one launch (start us, length us, event | category | flops | bytes accessed | tf_op | source)
XLA Modules:
  0.0 223.2 jit_solution(12558334718390605281)
XLA Ops:
  0.6 31.0 %sum_projected.1 = (bf16[192,512]{1,0:T(8,128)(2,1)}, f32[192,128]{1,0:T(8,128)}) custom-call(bf16[192,2048]{1,0:T(8,128)(2,1)} %bitcast.15, bf16[544,2048]{1,0:T(8,128)(2,1)} %bitcast.19), custom_call_target="tpu_custom_call" | custom-call | tf_op jit(solution)/shard_map/sum_projected/pallas_call | solution.py:480
  31.7 20.7 %first_pass.1 = (f32[16,24,8,128]{3,2,1,0:T(8,128)}, f32[192,2048]{1,0:T(8,128)}, f32[192,2048]{1,0:T(8,128)}, f32[16,24,8,128]{3,2,1,0:T(8,128)}, f32[16,24,8,1...) custom-call(bf16[192,512]{1,0:T(8,128)(2,1)} %get-tuple-element.37.l, ...), custom_call_target="tpu_custom_call" | custom-call | tf_op jit(solution)/shard_map/first_pass/pallas_call | solution.py:303
  52.3 18.8 %exchange.1.across_ref = f32[16,32,128]{2,1,0:T(8,128)} custom-call(f32[16,40,128]{2,1,0:T(8,128)} %get-tuple-element.47.pack_ref, f32[16,2048]{1,0:T(8,128)} %bitcast.28), custom_call_target="tpu_custom_call" | custom-call | tf_op jit(solution)/shard_map/exchange/pallas_call | solution.py:527
  71.2 36.7 %second_pass.1 = (bf16[192,2048]{1,0:T(8,128)(2,1)}, f32[192,2048]{1,0:T(8,128)}, f32[192,640]{1,0:T(8,128)}, bf16[2,4,2,2,16,2048]{5,4,3,2,1,0:T(8,128)(2,1)}, f32[16,24,128]{2,1,0:T(8,128)}) custom-call(bf16[192,512]{1,0:T(8,128)(2,1)} %get-tuple-element.37.low_ref, f32[192,128]{1,0:T(8,128)} %get-tuple-element.38.io_ref, bf16[512,2048]{1,0:T(8,128)(2,1)} %bitcast.22, ...), custom_call_target="tpu_custom_call" | custom-call | tf_op jit(solution)/shard_map/second_pass/pallas_call | solution.py:334
  107.9 45.6 %tail.1 = (bf16[192,2048]{1,0:T(8,128)(2,1)}, bf16[192,2048]{1,0:T(8,128)(2,1)}, f32[544,128]{1,0:T(8,128)}, f32[32,2048]{1,0:T(8,128)}, f32[16,2048]{1,0:T(8,12...) custom-call(f32[192,640]{1,0:T(8,128)} %get-tuple-element.48.part_ref, f32[16,24,128]{2,1,0:T(8,128)} %get-tuple-element.49.small_in, ...), custom_call_target="tpu_custom_call" | custom-call | tf_op jit(solution)/shard_map/tail/pallas_call | solution.py:788
  153.6 69.7 %finish.1 = (bf16[192,2048]{1,0:T(8,128)(2,1)}, bf16[192,2048]{1,0:T(8,128)(2,1)}, f32[544,128]{1,0:T(8,128)}, f32[32,2048]{1,0:T(8,128)}, f32[16,2048]{1,0:T(8,...) custom-call(bf16[192,2048]{1,0:T(8,128)(2,1)} %get-tuple-element.53.refs_0_, bf16[192,2048]{1,0:T(8,128)(2,1)} %get-tuple-element.54.refs_1_, ...), custom_call_target="tpu_custom_call" | custom-call | tf_op jit(solution)/shard_map/finish/pallas_call | solution.py:824

commit v3 on v2

--- a/solution.py
+++ b/solution.py
@@ -67,6 +67,11 @@
     lax.fori_loop(0, STEPS, one, 0)
 
 
+def inverse(value):
+    rough = pl.reciprocal(value, approx=True)
+    return rough * (2.0 - value * rough)
+
+
 def scan_rows(decay, value, reverse):
     row = row_index()
     for k in (1, 2, 4):
@@ -88,13 +93,16 @@
         spread_columns(io_ref, spread)
 
     pre = jnp.dot(low_ref[...], w_ref[...], preferred_element_type=F32) + bias_ref[...]
-    step = jnp.maximum(pre, 0.0) + jnp.log1p(jnp.exp(-jnp.abs(pre)))
-    sig_ref[...] = jax.nn.sigmoid(pre)
+    small = jnp.exp(-jnp.abs(pre))
+    above = inverse(1.0 + small)
+    series = small * (1.0 - small * (0.5 - small * (1.0 / 3.0)))
+    step = jnp.maximum(pre, 0.0) + jnp.where(small < 1e-3, series, jnp.log(1.0 + small))
+    sig_ref[...] = jnp.where(pre >= 0.0, above, small * above)
     z = z_ref[...].astype(F32)
     token_ref[...] = step
     by_step(step_ref, step, by_step_size)
     by_step(drive, step * u_ref[...].astype(F32), by_drive)
-    by_step(seed, g_ref[...].astype(F32) * z * jax.nn.sigmoid(z), by_seed)
+    by_step(seed, g_ref[...].astype(F32) * z * inverse(1.0 + jnp.exp(-z)), by_seed)
     rates[...] = -LOG2E * jnp.exp(dlog_ref[...])
     row = row_index()
 
@@ -126,7 +134,7 @@
 
         zero = tuple(jnp.zeros((ROWS, LANE), F32) for _ in pairs)
         ones = tuple(jnp.ones((ROWS, LANE), F32) for _ in pairs)
-        state, decay, start = lax.fori_loop(0, STEPS, one, (zero, ones, zero), unroll=4)
+        state, decay, start = lax.fori_loop(0, STEPS, one, (zero, ones, zero), unroll=12)
         for p, (n, k) in enumerate(pairs):
             ends = scan_rows(decay[p], state[p], False)
             starts = scan_rows(decay[p], start[p], True)
@@ -150,7 +158,7 @@
     low_ref, io_ref, w_ref, dlog_ref, skip_ref, u_ref, z_ref, g_ref, step_ref, token_ref, sig_ref, drive, seed,
     entry_ref, exit_ref, bsum_ref, across_ref,
     dgate_ref, dsig_ref, part_ref, gstep_ref, small_ref,
-    spread, sums, held, scanned, grad_drive, grad_decay, by_scan, by_grad, by_decay, rates, by_token,
+    spread, sums, held, scanned, grad_drive, grad_decay, by_scan, by_grad, by_decay, rates, by_token, low_t,
 ):
     tile = pl.program_id(0)
 
@@ -159,24 +167,27 @@
         spread_columns(io_ref, spread)
         sums[...] = jnp.zeros_like(sums)
         part_ref[...] = jnp.zeros_like(part_ref)
+        low_t[...] = low_ref[...].astype(F32).T.astype(BF16)
 
     rates[...] = -LOG2E * jnp.exp(dlog_ref[...])
-    scanned[...] = jnp.zeros_like(scanned)
-    grad_drive[...] = jnp.zeros_like(grad_drive)
-    grad_decay[...] = jnp.zeros_like(grad_decay)
     prior = sum_before(bsum_ref[...], False)
     later = sum_before(bsum_ref[...], True)
+
+    def so_far(ref, c, i):
+        if c == 0:
+            return [jnp.zeros((ROWS, LANE), F32) for k in range(HALVES)]
+        return [ref[k, i] for k in range(HALVES)]
 
     for c in range(N // CHUNK):
         numbers = range(c * CHUNK, (c + 1) * CHUNK)
         pairs = [(n, k) for n in numbers for k in range(HALVES)]
         rate = [jnp.broadcast_to(rates[n : n + 1, lanes(k)], (ROWS, LANE)) for n, k in pairs]
 
-        def forward(i, state):
+        def forward(i, state, c=c, numbers=numbers, rate=rate):
             st = [step_ref[k, i] for k in range(HALVES)]
             dr = [drive[k, i] for k in range(HALVES)]
             sd = [seed[k, i] for k in range(HALVES)]
-            out = [scanned[k, i] for k in range(HALVES)]
+            out = so_far(scanned, c, i)
             new = []
             for m, n in enumerate(numbers):
                 b_in, b_out = spread[i, n], spread[i, N + n]
@@ -198,16 +209,16 @@
             + jnp.exp2(prior[:, lanes(k)] * rate[p]) * across_ref[k, n : n + 1, :]
             for p, (n, k) in enumerate(pairs)
         )
-        lax.fori_loop(0, STEPS, forward, state, unroll=4)
-
-        def backward(j, carry):
+        lax.fori_loop(0, STEPS, forward, state, unroll=8)
+
+        def backward(j, carry, c=c, numbers=numbers, rate=rate):
             incoming, total = carry
             i = STEPS - 1 - j
             st = [step_ref[k, i] for k in range(HALVES)]
             dr = [drive[k, i] for k in range(HALVES)]
             sd = [seed[k, i] for k in range(HALVES)]
-            g_drive = [grad_drive[k, i] for k in range(HALVES)]
-            g_decay = [grad_decay[k, i] for k in range(HALVES)]
+            g_drive = so_far(grad_drive, c, i)
+            g_decay = so_far(grad_decay, c, i)
             new_in, new_total = [], []
             for m, n in enumerate(numbers):
                 b_in, b_out = spread[i, n], spread[i, N + n]
@@ -234,7 +245,7 @@
             for p, (n, k) in enumerate(pairs)
         )
         zero = tuple(jnp.zeros((ROWS, LANE), F32) for _ in pairs)
-        _, total = lax.fori_loop(0, STEPS, backward, (incoming, zero), unroll=4)
+        _, total = lax.fori_loop(0, STEPS, backward, (incoming, zero), unroll=8)
         for p, (n, k) in enumerate(pairs):
             small_ref[k, n : n + 1, :] = (
                 jnp.sum(total[p], axis=0, keepdims=True) * rates[n : n + 1, lanes(k)] * LN2
@@ -243,7 +254,7 @@
     u = u_ref[...].astype(F32)
     z = z_ref[...].astype(F32)
     g = g_ref[...].astype(F32)
-    gate_sig = jax.nn.sigmoid(z)
+    gate_sig = inverse(1.0 + jnp.exp(-z))
     seeds = g * z * gate_sig
     skip = skip_ref[...]
     from_drive = from_step(grad_drive, by_grad)
@@ -261,9 +272,7 @@
     part_ref[:, :R] += lax.dot_general(
         pre, w_ref[...], (((1,), (1,)), ((), ())), preferred_element_type=F32
     )
-    grad = lax.dot_general(
-        low_ref[...], pre, (((0,), (0,)), ((), ())), preferred_element_type=F32
-    ).astype(BF16)
+    grad = jnp.dot(low_t[...], pre, preferred_element_type=F32).astype(BF16)
     for x in range(SIDE):
         for y in range(SIDE):
             at = (x * SIDE + y) * 2 * 16
@@ -353,17 +362,21 @@
         ]
         + [pltpu.VMEM((HALVES, STEPS, ROWS, LANE), F32)] * 3
         + [pltpu.VMEM((HALVES, TOK, LANE), F32)] * 3
-        + [pltpu.VMEM((N, TILE), F32), pltpu.VMEM((TOK, LANE), F32)],
+        + [pltpu.VMEM((N, TILE), F32), pltpu.VMEM((TOK, LANE), F32), pltpu.VMEM((R, TOK), BF16)],
         compiler_params=pltpu.CompilerParams(vmem_limit_bytes=VMEM_BYTES),
         name="second_pass",
     )(low, io, weight, dlog, skip, u, z, g, *kept, across)
 
 
 def greet(partners):
-    barrier = pltpu.get_barrier_semaphore()
     for partner in partners:
-        pl.semaphore_signal(barrier, inc=1, device_id=partner, device_id_type=MESH)
-    pl.semaphore_wait(barrier, len(partners))
+        pl.semaphore_signal(
+            pltpu.get_barrier_semaphore(), inc=1, device_id=partner, device_id_type=MESH
+        )
+
+
+def met(partners):
+    pl.semaphore_wait(pltpu.get_barrier_semaphore(), len(partners))
 
 
 def remote(src, dst, send, recv, to):
@@ -395,11 +408,14 @@
     return jnp.concatenate([rows[:, : R // 2], rows[:, R // 2 : R]], axis=0)
 
 
-def sum_start(part_ref, low_part, io_part, low_land, io_land, send, recv):
+def prepare(part_ref, low_part, io_part):
     for p in range(CH):
         rows = part_ref[p * PIECE : (p + 1) * PIECE, :]
         low_part[p] = over(rows).astype(low_part.dtype)
         io_part[p] = fold(rows[:, R:])
+
+
+def sum_start(low_part, io_part, low_land, io_land, send, recv):
     copies = []
     for d, to in enumerate(others("ch", CH)):
         copies.append(remote(low_part.at[to["ch"]], low_land.at[d], send.at[0, d], recv.at[0, d], to))
@@ -458,12 +474,14 @@
 
 def sum_projected(u_ref, xt_ref, low_ref, io_ref, part_ref, *scratch):
     low_part, io_part, low_land, io_land, low_all, io_all, wide, sum_send, sum_recv, all_send, all_recv = scratch
+    greet(others("ch", CH))
     part_ref[:, R:] = jnp.zeros((TOK, LANE), F32)
     part_ref[:, : R + 2 * N] = lax.dot_general(
         u_ref[...], xt_ref[...], (((1,), (1,)), ((), ())), preferred_element_type=F32
     )
-    greet(others("ch", CH))
-    sums = sum_start(part_ref, low_part, io_part, low_land, io_land, sum_send, sum_recv)
+    prepare(part_ref, low_part, io_part)
+    met(others("ch", CH))
+    sums = sum_start(low_part, io_part, low_land, io_land, sum_send, sum_recv)
     shares = share_start(sums, part_ref, io_part, low_land, io_land, low_all, io_all, all_send, all_recv)
     share_finish(shares, low_all, io_all, wide)
     low_ref[...] = wide[:, :R].astype(BF16)
@@ -503,6 +521,7 @@
 def exchange(pack_ref, dlog_ref, out_ref, landed, back, result, send, recv, back_send, back_recv):
     me = lax.axis_index("ctx")
     greet(others("ctx", CTX))
+    met(others("ctx", CTX))
     there = spread_start(pack_ref, landed, send, recv)
     rates = -jnp.exp(dlog_ref[:, pl.ds(pl.multiple_of(me * LANE, LANE), LANE)])
     for copy in there:
@@ -670,11 +689,12 @@
 
 
 def tail(
-    part_ref, small_in, dgate_ref, step_grad, u_ref, xw_ref, dsig_ref,
+    part_ref, small_in, dgate_ref, step_grad, u_hbm, xw_hbm, dsig_hbm,
     hin_ref, hgate_ref, gx_ref, gstep_ref, gdecay_ref, gbias_ref, gskip_ref,
     low_part, io_part, low_land, io_land, low_all, io_all, wide, sum_send, sum_recv, all_send, all_recv,
     small_land, small_back, small_all, s_send, s_recv, t_send, t_recv,
-    gate_land, in_out, in_land, hand_send, hand_recv, proj, proj_t, x_grad0, x_grad1, *scratch,
+    gate_land, in_out, in_land, hand_send, hand_recv, proj, proj_t, x_grad0, x_grad1,
+    u_ref, xw_ref, dsig_ref, load_sem, *scratch,
 ):
     rings = [scratch[k * RING : (k + 1) * RING] for k in range(4)]
     step_ring, x_ring = rings[:2], rings[2:]
@@ -682,11 +702,20 @@
     x_grad = [x_grad0, x_grad1]
     section = lax.axis_index("section")
     me = lax.axis_index("ctx")
-    greet(others("ctx", CTX) + others("ch", CH) + [{"section": 1 - section}])
+    partners = others("ctx", CTX) + others("ch", CH) + [{"section": 1 - section}]
+    greet(partners)
+    loads = [
+        pltpu.make_async_copy(src, dst, load_sem.at[k])
+        for k, (src, dst) in enumerate(((u_hbm, u_ref), (xw_hbm, xw_ref), (dsig_hbm, dsig_ref)))
+    ]
+    for load in loads:
+        load.start()
+    prepare(part_ref, low_part, io_part)
+    met(partners)
     gate_copy = remote(dgate_ref, gate_land, hand_send.at[0], hand_recv.at[0], {"section": 1 - section})
     in_copy = remote(in_out, in_land, hand_send.at[1], hand_recv.at[1], {"section": 1 - section})
 
-    sums = sum_start(part_ref, low_part, io_part, low_land, io_land, sum_send, sum_recv)
+    sums = sum_start(low_part, io_part, low_land, io_land, sum_send, sum_recv)
     first = plane_start(step_grad, step_ring)
 
     @pl.when(section == 1)
@@ -711,6 +740,9 @@
     proj[...] = wide[...].astype(BF16)
     proj_t[...] = wide[...].T.astype(BF16)
 
+    for load in loads:
+        load.wait()
+
     def product(c, _):
         columns = pl.ds(pl.multiple_of(c * TILE, TILE), TILE)
         grad = jnp.dot(
@@ -787,7 +819,7 @@
     b = lambda *s: jax.ShapeDtypeStruct(s, BF16)
     return pl.pallas_call(
         tail,
-        in_specs=in_vmem(7),
+        in_specs=in_vmem(4) + [pl.BlockSpec(memory_space=pl.ANY)] * 3,
         out_specs=in_vmem(7),
         out_shape=[
             b(TOK, ch), b(TOK, ch), f(R + 2 * N, LANE), f(32, ch), f(N, ch), f(1, ch), f(1, ch),
@@ -799,6 +831,8 @@
         + [pltpu.SemaphoreType.DMA((2,))] * 2
         + [pltpu.VMEM((TOK, WIDE), BF16), pltpu.VMEM((WIDE, TOK), BF16)]
         + [pltpu.VMEM((SIDE, 2, 2, rows, LANE), BF16) for rows in X_ROWS]
+        + [pltpu.VMEM(u.shape, BF16), pltpu.VMEM(xw.shape, BF16), pltpu.VMEM(dsig.shape, F32)]
+        + [pltpu.SemaphoreType.DMA((3,))]
         + ring_scratch((2, 16, 2048), (16, 1024)) * 2
         + ring_scratch((2, X_ROWS[0], LANE), (X_ROWS[0] // 2, LANE))
         + ring_scratch((2, X_ROWS[1], LANE), (X_ROWS[1] // 2, LANE)),
@@ -811,22 +845,16 @@
 
 def finish(*refs):
     count = len(refs) // 2
-    sem = refs[-1]
-    copies = [pltpu.make_async_copy(refs[k], refs[count + k], sem.at[k]) for k in range(count)]
-    for copy in copies:
-        copy.start()
-    for copy in copies:
-        copy.wait()
+    for k in range(count):
+        refs[count + k][...] = refs[k][...]
 
 
 def run_finish(*results):
-    anywhere = [pl.BlockSpec(memory_space=pl.ANY)] * len(results)
     return pl.pallas_call(
         finish,
-        in_specs=anywhere,
-        out_specs=anywhere,
+        in_specs=in_vmem(len(results)),
+        out_specs=in_vmem(len(results)),
         out_shape=[jax.ShapeDtypeStruct(r.shape, r.dtype) for r in results],
-        scratch_shapes=[pltpu.SemaphoreType.DMA((len(results),))],
         compiler_params=pltpu.CompilerParams(vmem_limit_bytes=VMEM_BYTES),
         name="finish",
     )(*results)

time: 223 us -> 154 us (0.69)
  Pallas kernels: 223 us -> 153 us
    pallas_call x2, Pallas kernels: 115 us -> 47.4 us  [the longest x1 44.4 us: run_tail(): pl.pallas_call(tail, in_specs=in_vmem(4) + [pl.BlockSpec(memory_space=pl....]
where the time goes in v3:
time: 154 us
  Pallas kernels  153 us (99%)
    pallas_call x1, Pallas kernels, run_tail(): pl.pallas_call(tail, in_specs=in_vmem(4) + [pl.BlockSpec(memory_space=pl....  44.4 us
    pallas_call x1, Pallas kernels, run_second(): pl.pallas_call(second_pass, grid=(ch // TILE,), in_specs=[whole(TOK, R),...  36.1 us
    pallas_call x1, Pallas kernels, run_sum(): pl.pallas_call(sum_projected, in_specs=in_vmem(2), out_specs=in_vmem(2),...  29.7 us
    pallas_call x1, Pallas kernels, run_first(): pl.pallas_call(first_pass, grid=(ch // TILE,), in_specs=[whole(TOK, R), w...  20.6 us
    pallas_call x1, Pallas kernels, run_exchange(): pl.pallas_call(exchange, in_specs=in_vmem(2), out_specs=pl.BlockSpec(memo...  19 us

profile of v3, /device:TPU:2, one launch (start us, length us, event | category | flops | bytes accessed | tf_op | source)
XLA Modules:
  0.0 153.5 jit_solution(8029930545186900941)
XLA Ops:
  0.6 29.7 %sum_projected.1 = (bf16[192,512]{1,0:T(8,128)(2,1)}, f32[192,128]{1,0:T(8,128)}) custom-call(bf16[192,2048]{1,0:T(8,128)(2,1)} %bitcast.15, bf16[544,2048]{1,0:T(8,128)(2,1)} %bitcast.19), custom_call_target="tpu_custom_call" | custom-call | tf_op jit(solution)/shard_map/sum_projected/pallas_call | solution.py:498
  30.4 20.6 %first_pass.1 = (f32[16,24,8,128]{3,2,1,0:T(8,128)}, f32[192,2048]{1,0:T(8,128)}, f32[192,2048]{1,0:T(8,128)}, f32[16,24,8,128]{3,2,1,0:T(8,128)}, f32[16,24,8,1...) custom-call(bf16[192,512]{1,0:T(8,128)(2,1)} %get-tuple-element.37.l, ...), custom_call_target="tpu_custom_call" | custom-call | tf_op jit(solution)/shard_map/first_pass/pallas_call | solution.py:312
  50.9 19.0 %exchange.1.across_ref = f32[16,32,128]{2,1,0:T(8,128)} custom-call(f32[16,40,128]{2,1,0:T(8,128)} %get-tuple-element.47.pack_ref, f32[16,2048]{1,0:T(8,128)} %bitcast.28), custom_call_target="tpu_custom_call" | custom-call | tf_op jit(solution)/shard_map/exchange/pallas_call | solution.py:546
  69.9 36.1 %second_pass.1 = (bf16[192,2048]{1,0:T(8,128)(2,1)}, f32[192,2048]{1,0:T(8,128)}, f32[192,640]{1,0:T(8,128)}, bf16[2,4,2,2,16,2048]{5,4,3,2,1,0:T(8,128)(2,1)}, f32[16,24,128]{2,1,0:T(8,128)}) custom-call(bf16[192,512]{1,0:T(8,128)(2,1)} %get-tuple-element.37.low_ref, f32[192,128]{1,0:T(8,128)} %get-tuple-element.38.io_ref, bf16[512,2048]{1,0:T(8,128)(2,1)} %bitcast.22, ...), custom_call_target="tpu_custom_call" | custom-call | tf_op jit(solution)/shard_map/second_pass/pallas_call | solution.py:343
  106.1 44.4 %tail.1 = (bf16[192,2048]{1,0:T(8,128)(2,1)}, bf16[192,2048]{1,0:T(8,128)(2,1)}, f32[544,128]{1,0:T(8,128)}, f32[32,2048]{1,0:T(8,128)}, f32[16,2048]{1,0:T(8,12...) custom-call(f32[192,640]{1,0:T(8,128)} %get-tuple-element.48.part_ref, f32[16,24,128]{2,1,0:T(8,128)} %get-tuple-element.49.small_in, ...), custom_call_target="tpu_custom_call" | custom-call | tf_op jit(solution)/shard_map/tail/pallas_call | solution.py:820
  150.5 3.0 %finish.1 = (bf16[192,2048]{1,0:T(8,128)(2,1)}, bf16[192,2048]{1,0:T(8,128)(2,1)}, f32[544,128]{1,0:T(8,128)}, f32[32,2048]{1,0:T(8,128)}, f32[16,2048]{1,0:T(8,...) custom-call(bf16[192,2048]{1,0:T(8,128)(2,1)} %get-tuple-element.53.refs_0_, bf16[192,2048]{1,0:T(8,128)(2,1)} %get-tuple-element.54.refs_1_, ...), custom_call_target="tpu_custom_call" | custom-call | tf_op jit(solution)/shard_map/finish/pallas_call | solution.py:853

commit v4 on v3

--- a/solution.py
+++ b/solution.py
@@ -16,7 +16,6 @@
 LANE = 128
 HALVES = TILE // LANE
 CHUNK = 4
-LOG2E = 1.4426950408889634
 VMEM_BYTES = 60 * 2**20
 SIDE = 4
 CTX = 16
@@ -26,7 +25,6 @@
 PACK = 40
 SMALL = 24
 MESH = pl.DeviceIdType.MESH
-LN2 = 0.6931471805599453
 F32 = jnp.float32
 BF16 = jnp.bfloat16
 
@@ -84,12 +82,17 @@
 
 
 def first_pass(
-    low_ref, io_ref, w_ref, bias_ref, dlog_ref, u_ref, z_ref, g_ref,
-    step_ref, token_ref, sig_ref, drive, seed, entry_ref, exit_ref, pack_ref, bsum_ref,
+    low_ref, io_ref, w_ref, bias_ref, dlog_ref, all_dlog_ref, u_ref, z_ref, g_ref,
+    step_ref, token_ref, sig_ref, drive, seed, decay_ref, entry_ref, exit_ref, bsum_ref, across_ref,
     spread, by_drive, by_seed, by_step_size, rates,
+    pack, landed, back, result, send, recv, back_send, back_recv,
 ):
-    @pl.when(pl.program_id(0) == 0)
+    tile = pl.program_id(0)
+    last = pl.num_programs(0) - 1
+    me = lax.axis_index("ctx")
+    @pl.when(tile == 0)
     def _():
+        greet(others("ctx", CTX))
         spread_columns(io_ref, spread)
 
     pre = jnp.dot(low_ref[...], w_ref[...], preferred_element_type=F32) + bias_ref[...]
@@ -103,7 +106,7 @@
     by_step(step_ref, step, by_step_size)
     by_step(drive, step * u_ref[...].astype(F32), by_drive)
     by_step(seed, g_ref[...].astype(F32) * z * inverse(1.0 + jnp.exp(-z)), by_seed)
-    rates[...] = -LOG2E * jnp.exp(dlog_ref[...])
+    rates[...] = -jnp.exp(dlog_ref[...])
     row = row_index()
 
     total = jnp.zeros((ROWS, TILE), F32)
@@ -112,7 +115,7 @@
     bsum_ref[...] = total
     whole_sum = jnp.sum(total, axis=0, keepdims=True)
     for k in range(HALVES):
-        pack_ref[k, 2 * N :, :] = jnp.broadcast_to(whole_sum[:, lanes(k)], (PACK - 2 * N, LANE))
+        pack[HALVES * tile + k, 2 * N :, :] = jnp.broadcast_to(whole_sum[:, lanes(k)], (PACK - 2 * N, LANE))
 
     for c in range(N // CHUNK):
         pairs = [(n, k) for n in range(c * CHUNK, (c + 1) * CHUNK) for k in range(HALVES)]
@@ -125,7 +128,8 @@
             sd = [seed[k, i] for k in range(HALVES)]
             new_state, new_decay, new_start = [], [], []
             for p, (n, k) in enumerate(pairs):
-                a = jnp.exp2(st[k] * rate[p])
+                a = jnp.exp(st[k] * rate[p])
+                decay_ref[k, i, n] = a
                 new_state.append(a * state[p] + dr[k] * spread[i, n])
                 d = a * decay[p]
                 new_decay.append(d)
@@ -140,8 +144,67 @@
             starts = scan_rows(decay[p], start[p], True)
             entry_ref[n, :, lanes(k)] = jnp.where(row >= 1, pltpu.roll(ends, 1, 0), 0.0)
             exit_ref[n, :, lanes(k)] = jnp.where(row < ROWS - 1, pltpu.roll(starts, ROWS - 1, 0), 0.0)
-            pack_ref[k, n : n + 1, :] = ends[ROWS - 1 :, :]
-            pack_ref[k, N + n : N + n + 1, :] = starts[:1, :]
+            pack[HALVES * tile + k, n : n + 1, :] = ends[ROWS - 1 :, :]
+            pack[HALVES * tile + k, N + n : N + n + 1, :] = starts[:1, :]
+
+    @pl.when(tile == 0)
+    def _():
+        met(others("ctx", CTX))
+
+    def chunk_to(c):
+        return remote(pack.at[c], landed.at[me], send.at[c], recv.at[me], {"ctx": c})
+
+    def chunk_from(c):
+        return remote(pack.at[c], landed.at[c], send.at[c], recv.at[c], {"ctx": c})
+
+    def answers():
+        return [
+            remote(back.at[to["ctx"]], result.at[me], back_send.at[d], back_recv.at[d], to)
+            for d, to in enumerate(others("ctx", CTX))
+        ]
+
+    for k in range(HALVES):
+        c = HALVES * tile + k
+
+        @pl.when(c != me)
+        def _():
+            chunk_to(c).start()
+
+        @pl.when(c == me)
+        def _():
+            landed[me] = pack[me]
+
+    @pl.when(tile == jnp.minimum(me // HALVES + 1, last))
+    def _():
+        for c in range(CTX):
+            @pl.when(c != me)
+            def _():
+                chunk_from(c).wait_recv()
+
+        mine = -jnp.exp(all_dlog_ref[:, pl.ds(pl.multiple_of(me * LANE, LANE), LANE)])
+        state = jnp.zeros((N, LANE), F32)
+        adjoint = jnp.zeros((N, LANE), F32)
+        for c in range(CTX):
+            r = CTX - 1 - c
+            back[c, :N] = state
+            back[r, N:] = adjoint
+            state = jnp.exp(landed[c, 2 * N : 2 * N + 1] * mine) * state + landed[c, :N]
+            adjoint = jnp.exp(landed[r, 2 * N : 2 * N + 1] * mine) * adjoint + landed[r, N : 2 * N]
+        result[me] = back[me]
+        for copy in answers():
+            copy.start()
+
+    @pl.when(tile == last)
+    def _():
+        for copy in answers():
+            copy.wait_recv()
+        across_ref[...] = result[...]
+        for copy in answers():
+            copy.wait_send()
+        for c in range(CTX):
+            @pl.when(c != me)
+            def _():
+                chunk_to(c).wait_send()
 
 
 def sum_before(value, reverse):
@@ -155,7 +218,7 @@
 
 
 def second_pass(
-    low_ref, io_ref, w_ref, dlog_ref, skip_ref, u_ref, z_ref, g_ref, step_ref, token_ref, sig_ref, drive, seed,
+    low_ref, io_ref, w_ref, dlog_ref, skip_ref, u_ref, z_ref, g_ref, step_ref, token_ref, sig_ref, drive, seed, decay_ref,
     entry_ref, exit_ref, bsum_ref, across_ref,
     dgate_ref, dsig_ref, part_ref, gstep_ref, small_ref,
     spread, sums, held, scanned, grad_drive, grad_decay, by_scan, by_grad, by_decay, rates, by_token, low_t,
@@ -169,7 +232,7 @@
         part_ref[...] = jnp.zeros_like(part_ref)
         low_t[...] = low_ref[...].astype(F32).T.astype(BF16)
 
-    rates[...] = -LOG2E * jnp.exp(dlog_ref[...])
+    rates[...] = -jnp.exp(dlog_ref[...])
     prior = sum_before(bsum_ref[...], False)
     later = sum_before(bsum_ref[...], True)
 
@@ -184,7 +247,6 @@
         rate = [jnp.broadcast_to(rates[n : n + 1, lanes(k)], (ROWS, LANE)) for n, k in pairs]
 
         def forward(i, state, c=c, numbers=numbers, rate=rate):
-            st = [step_ref[k, i] for k in range(HALVES)]
             dr = [drive[k, i] for k in range(HALVES)]
             sd = [seed[k, i] for k in range(HALVES)]
             out = so_far(scanned, c, i)
@@ -195,7 +257,7 @@
                 for k in range(HALVES):
                     p = m * HALVES + k
                     held[i, m, :, lanes(k)] = state[p]
-                    now = jnp.exp2(st[k] * rate[p]) * state[p] + dr[k] * b_in
+                    now = decay_ref[k, i, n] * state[p] + dr[k] * b_in
                     new.append(now)
                     out[k] = out[k] + b_out * now
                     d_out = d_out + sd[k] * now
@@ -206,7 +268,7 @@
 
         state = tuple(
             entry_ref[n, :, lanes(k)]
-            + jnp.exp2(prior[:, lanes(k)] * rate[p]) * across_ref[k, n : n + 1, :]
+            + jnp.exp(prior[:, lanes(k)] * rate[p]) * across_ref[k, n : n + 1, :]
             for p, (n, k) in enumerate(pairs)
         )
         lax.fori_loop(0, STEPS, forward, state, unroll=8)
@@ -226,7 +288,7 @@
                 for k in range(HALVES):
                     p = m * HALVES + k
                     adjoint = b_out * sd[k] + incoming[p]
-                    passed = jnp.exp2(st[k] * rate[p]) * adjoint
+                    passed = decay_ref[k, i, n] * adjoint
                     pulled = passed * held[i, m, :, lanes(k)]
                     new_in.append(passed)
                     new_total.append(total[p] + pulled * st[k])
@@ -241,14 +303,14 @@
 
         incoming = tuple(
             exit_ref[n, :, lanes(k)]
-            + jnp.exp2(later[:, lanes(k)] * rate[p]) * across_ref[k, N + n : N + n + 1, :]
+            + jnp.exp(later[:, lanes(k)] * rate[p]) * across_ref[k, N + n : N + n + 1, :]
             for p, (n, k) in enumerate(pairs)
         )
         zero = tuple(jnp.zeros((ROWS, LANE), F32) for _ in pairs)
         _, total = lax.fori_loop(0, STEPS, backward, (incoming, zero), unroll=8)
         for p, (n, k) in enumerate(pairs):
             small_ref[k, n : n + 1, :] = (
-                jnp.sum(total[p], axis=0, keepdims=True) * rates[n : n + 1, lanes(k)] * LN2
+                jnp.sum(total[p], axis=0, keepdims=True) * rates[n : n + 1, lanes(k)]
             )
 
     u = u_ref[...].astype(F32)
@@ -261,7 +323,7 @@
     mixed = from_step(scanned, by_scan) + skip * u
     dgate_ref[...] = (g * mixed * gate_sig * (1.0 + z * (1.0 - gate_sig))).astype(BF16)
     dsig_ref[...] = from_drive * token_ref[...] + skip * seeds
-    d_pre = (from_drive * u + from_step(grad_decay, by_decay) * LN2) * sig_ref[...]
+    d_pre = (from_drive * u + from_step(grad_decay, by_decay)) * sig_ref[...]
     pre = d_pre.astype(BF16)
     bias_row = jnp.sum(d_pre, axis=0, keepdims=True)
     skip_row = jnp.sum(seeds * u, axis=0, keepdims=True)
@@ -313,17 +375,18 @@
         first_pass,
         grid=(ch // TILE,),
         in_specs=[
-            whole(TOK, R), whole(TOK, io.shape[1]), tiled(R), tiled(1), tiled(N),
+            whole(TOK, R), whole(TOK, io.shape[1]), tiled(R), tiled(1), tiled(N), whole(N, ch),
             tiled(TOK), tiled(TOK), tiled(TOK),
         ],
         out_specs=[
             stacked(STEPS, ROWS), tiled(TOK), tiled(TOK), stacked(STEPS, ROWS), stacked(STEPS, ROWS),
-            tiled(N, ROWS), tiled(N, ROWS), stacked(PACK), tiled(ROWS),
+            stacked(STEPS, N, ROWS), tiled(N, ROWS), tiled(N, ROWS), tiled(ROWS), whole(CTX, 2 * N, LANE),
         ],
         out_shape=[
             f(ch // LANE, STEPS, ROWS, LANE), f(TOK, ch), f(TOK, ch), f(ch // LANE, STEPS, ROWS, LANE),
-            f(ch // LANE, STEPS, ROWS, LANE), f(N, ROWS, ch), f(N, ROWS, ch),
-            f(ch // LANE, PACK, LANE), f(ROWS, ch),
+            f(ch // LANE, STEPS, ROWS, LANE), f(ch // LANE, STEPS, N, ROWS, LANE),
+            f(N, ROWS, ch), f(N, ROWS, ch),
+            f(ROWS, ch), f(CTX, 2 * N, LANE),
         ],
         scratch_shapes=[
             pltpu.VMEM((STEPS, 2 * N, ROWS, LANE), F32),
@@ -331,10 +394,20 @@
             pltpu.VMEM((HALVES, TOK, LANE), F32),
             pltpu.VMEM((HALVES, TOK, LANE), F32),
             pltpu.VMEM((N, TILE), F32),
+            pltpu.VMEM((CTX, PACK, LANE), F32),
+            pltpu.VMEM((CTX, PACK, LANE), F32),
+            pltpu.VMEM((CTX, 2 * N, LANE), F32),
+            pltpu.VMEM((CTX, 2 * N, LANE), F32),
+            pltpu.SemaphoreType.DMA((CTX,)),
+            pltpu.SemaphoreType.DMA((CTX,)),
+            pltpu.SemaphoreType.DMA((CTX - 1,)),
+            pltpu.SemaphoreType.DMA((CTX - 1,)),
         ],
-        compiler_params=pltpu.CompilerParams(vmem_limit_bytes=VMEM_BYTES),
+        compiler_params=pltpu.CompilerParams(
+            collective_id=1, has_side_effects=True, vmem_limit_bytes=VMEM_BYTES
+        ),
         name="first_pass",
-    )(low, io, weight, bias, dlog, u, z, g)
+    )(low, io, weight, bias, dlog, dlog, u, z, g)
 
 
 def run_second(low, io, weight, dlog, skip, u, z, g, kept, across):
@@ -346,7 +419,7 @@
         in_specs=[
             whole(TOK, R), whole(TOK, io.shape[1]), tiled(R), tiled(N), tiled(1),
             tiled(TOK), tiled(TOK), tiled(TOK), stacked(STEPS, ROWS), tiled(TOK), tiled(TOK),
-            stacked(STEPS, ROWS), stacked(STEPS, ROWS), tiled(N, ROWS), tiled(N, ROWS), tiled(ROWS), stacked(2 * N),
+            stacked(STEPS, ROWS), stacked(STEPS, ROWS), stacked(STEPS, N, ROWS), tiled(N, ROWS), tiled(N, ROWS), tiled(ROWS), stacked(2 * N),
         ],
         out_specs=[
             tiled(TOK), tiled(TOK), whole(TOK, WIDE), tiled(2, SIDE, 2, 2, 16), stacked(SMALL),
@@ -516,49 +589,6 @@
         copies[-1].start()
     dst[me] = src[me]
     return copies
-
-
-def exchange(pack_ref, dlog_ref, out_ref, landed, back, result, send, recv, back_send, back_recv):
-    me = lax.axis_index("ctx")
-    greet(others("ctx", CTX))
-    met(others("ctx", CTX))
-    there = spread_start(pack_ref, landed, send, recv)
-    rates = -jnp.exp(dlog_ref[:, pl.ds(pl.multiple_of(me * LANE, LANE), LANE)])
-    for copy in there:
-        copy.wait_recv()
-    state = jnp.zeros((N, LANE), F32)
-    adjoint = jnp.zeros((N, LANE), F32)
-    for c in range(CTX):
-        r = CTX - 1 - c
-        back[c, :N] = state
-        back[r, N:] = adjoint
-        state = jnp.exp(landed[c, 2 * N : 2 * N + 1] * rates) * state + landed[c, :N]
-        adjoint = jnp.exp(landed[r, 2 * N : 2 * N + 1] * rates) * adjoint + landed[r, N : 2 * N]
-    home = spread_start(back, result, back_send, back_recv)
-    for copy in home:
-        copy.wait_recv()
-    out_ref[...] = result[...]
-    for copy in there + home:
-        copy.wait_send()
-
-
-def run_exchange(pack, dlog):
-    return pl.pallas_call(
-        exchange,
-        in_specs=in_vmem(2),
-        out_specs=pl.BlockSpec(memory_space=pltpu.VMEM),
-        out_shape=jax.ShapeDtypeStruct((CTX, 2 * N, LANE), F32),
-        scratch_shapes=[
-            pltpu.VMEM((CTX, PACK, LANE), F32),
-            pltpu.VMEM((CTX, 2 * N, LANE), F32),
-            pltpu.VMEM((CTX, 2 * N, LANE), F32),
-        ]
-        + [pltpu.SemaphoreType.DMA((CTX - 1,))] * 4,
-        compiler_params=pltpu.CompilerParams(
-            collective_id=1, has_side_effects=True, vmem_limit_bytes=VMEM_BYTES
-        ),
-        name="exchange",
-    )(pack, dlog)
 
 
 def neighbour(axis, d):
@@ -865,10 +895,9 @@
     weight_x, weight_step = jnp.swapaxes(x_weight[0], 0, 1), step_weight[0]
     dlog = decay_log[0]
     low, io = run_sum(u, weight_x)
-    *kept, pack, bsum = run_first(low, io, weight_step, step_bias, dlog, u, z, g)
-    across = run_exchange(pack, dlog)
+    *kept, across = run_first(low, io, weight_step, step_bias, dlog, u, z, g)
     d_gate, d_signal, d_part, grad_step, small = run_second(
-        low, io, weight_step, dlog, skip_gain, u, z, g, [*kept, bsum], across
+        low, io, weight_step, dlog, skip_gain, u, z, g, kept, across
     )
     handed_input, handed_gate, grad_x, grad_step, g_decay, g_bias, g_skip = run_finish(
         *run_tail(d_part, small, d_gate, grad_step, u, weight_x, d_signal)

time: 154 us -> 153 us (level)
    pallas_call x1, Pallas kernels: 20.6 us -> 41 us  [run_first(): pl.pallas_call(first_pass, grid=(ch // TILE,), in_specs=[whole(TOK, R), w...]
    pallas_call x1 -> x0, Pallas kernels: 19 us -> none  [run_exchange(): pl.pallas_call(exchange, in_specs=in_vmem(2), out_specs=pl.BlockSpec(memo...]
where the time goes in v4:
time: 153 us
  Pallas kernels  152 us (99%)
    pallas_call x1, Pallas kernels, run_tail(): pl.pallas_call(tail, in_specs=in_vmem(4) + [pl.BlockSpec(memory_space=pl....  43.4 us
    pallas_call x1, Pallas kernels, run_first(): pl.pallas_call(first_pass, grid=(ch // TILE,), in_specs=[whole(TOK, R), w...  41 us
    pallas_call x1, Pallas kernels, run_second(): pl.pallas_call(second_pass, grid=(ch // TILE,), in_specs=[whole(TOK, R),...  34.9 us
    pallas_call x1, Pallas kernels, run_sum(): pl.pallas_call(sum_projected, in_specs=in_vmem(2), out_specs=in_vmem(2),...  29.7 us

profile of v4, /device:TPU:2, one launch (start us, length us, event | category | flops | bytes accessed | tf_op | source)
XLA Modules:
  0.0 152.7 jit_solution(17308260601230643423)
XLA Ops:
  0.6 29.7 %sum_projected.1 = (bf16[192,512]{1,0:T(8,128)(2,1)}, f32[192,128]{1,0:T(8,128)}) custom-call(bf16[192,2048]{1,0:T(8,128)(2,1)} %bitcast.15, bf16[544,2048]{1,0:T(8,128)(2,1)} %bitcast.19), custom_call_target="tpu_custom_call" | custom-call | tf_op jit(solution)/shard_map/sum_projected/pallas_call | solution.py:571
  30.4 41.0 %first_pass.1 = (f32[16,24,8,128]{3,2,1,0:T(8,128)}, f32[192,2048]{1,0:T(8,128)}, f32[192,2048]{1,0:T(8,128)}, f32[16,24,8,128]{3,2,1,0:T(8,128)}, f32[16,24,8,1...) custom-call(bf16[192,512]{1,0:T(8,128)(2,1)} %get-tuple-element.38.l, ...), custom_call_target="tpu_custom_call" | custom-call | tf_op jit(solution)/shard_map/first_pass/pallas_call | solution.py:374
  71.4 34.9 %second_pass.1 = (bf16[192,2048]{1,0:T(8,128)(2,1)}, f32[192,2048]{1,0:T(8,128)}, f32[192,640]{1,0:T(8,128)}, bf16[2,4,2,2,16,2048]{5,4,3,2,1,0:T(8,128)(2,1)}, f32[16,24,128]{2,1,0:T(8,128)}) custom-call(bf16[192,512]{1,0:T(8,128)(2,1)} %get-tuple-element.38.low_ref, f32[192,128]{1,0:T(8,128)} %get-tuple-element.39.io_ref, bf16[512,2048]{1,0:T(8,128)(2,1)} %bitcast.22, ...), custom_call_target="tpu_custom_call" | custom-call | tf_op jit(solution)/shard_map/second_pass/pallas_call | solution.py:416
  106.3 43.4 %tail.1 = (bf16[192,2048]{1,0:T(8,128)(2,1)}, bf16[192,2048]{1,0:T(8,128)(2,1)}, f32[544,128]{1,0:T(8,128)}, f32[32,2048]{1,0:T(8,128)}, f32[16,2048]{1,0:T(8,12...) custom-call(f32[192,640]{1,0:T(8,128)} %get-tuple-element.50.part_ref, f32[16,24,128]{2,1,0:T(8,128)} %get-tuple-element.51.small_in, ...), custom_call_target="tpu_custom_call" | custom-call | tf_op jit(solution)/shard_map/tail/pallas_call | solution.py:850
  149.7 3.0 %finish.1 = (bf16[192,2048]{1,0:T(8,128)(2,1)}, bf16[192,2048]{1,0:T(8,128)(2,1)}, f32[544,128]{1,0:T(8,128)}, f32[32,2048]{1,0:T(8,128)}, f32[16,2048]{1,0:T(8,...) custom-call(bf16[192,2048]{1,0:T(8,128)(2,1)} %get-tuple-element.55.refs_0_, bf16[192,2048]{1,0:T(8,128)(2,1)} %get-tuple-element.56.refs_1_, ...), custom_call_target="tpu_custom_call" | custom-call | tf_op jit(solution)/shard_map/finish/pallas_call | solution.py:883

commit v5 on v4

--- a/solution.py
+++ b/solution.py
@@ -83,7 +83,7 @@
 
 def first_pass(
     low_ref, io_ref, w_ref, bias_ref, dlog_ref, all_dlog_ref, u_ref, z_ref, g_ref,
-    step_ref, token_ref, sig_ref, drive, seed, decay_ref, entry_ref, exit_ref, bsum_ref, across_ref,
+    step_ref, token_ref, sig_ref, drive, seed, entry_ref, exit_ref, bsum_ref, across_ref,
     spread, by_drive, by_seed, by_step_size, rates,
     pack, landed, back, result, send, recv, back_send, back_recv,
 ):
@@ -129,7 +129,6 @@
             new_state, new_decay, new_start = [], [], []
             for p, (n, k) in enumerate(pairs):
                 a = jnp.exp(st[k] * rate[p])
-                decay_ref[k, i, n] = a
                 new_state.append(a * state[p] + dr[k] * spread[i, n])
                 d = a * decay[p]
                 new_decay.append(d)
@@ -218,10 +217,10 @@
 
 
 def second_pass(
-    low_ref, io_ref, w_ref, dlog_ref, skip_ref, u_ref, z_ref, g_ref, step_ref, token_ref, sig_ref, drive, seed, decay_ref,
+    low_ref, io_ref, w_ref, dlog_ref, skip_ref, u_ref, z_ref, g_ref, step_ref, token_ref, sig_ref, drive, seed,
     entry_ref, exit_ref, bsum_ref, across_ref,
     dgate_ref, dsig_ref, part_ref, gstep_ref, small_ref,
-    spread, sums, held, scanned, grad_drive, grad_decay, by_scan, by_grad, by_decay, rates, by_token, low_t,
+    spread, sums, held, decays, scanned, grad_drive, grad_decay, by_scan, by_grad, by_decay, rates, by_token, low_t,
 ):
     tile = pl.program_id(0)
 
@@ -247,6 +246,7 @@
         rate = [jnp.broadcast_to(rates[n : n + 1, lanes(k)], (ROWS, LANE)) for n, k in pairs]
 
         def forward(i, state, c=c, numbers=numbers, rate=rate):
+            st = [step_ref[k, i] for k in range(HALVES)]
             dr = [drive[k, i] for k in range(HALVES)]
             sd = [seed[k, i] for k in range(HALVES)]
             out = so_far(scanned, c, i)
@@ -256,8 +256,10 @@
                 d_out = sums[i, N + n]
                 for k in range(HALVES):
                     p = m * HALVES + k
-                    held[i, m, :, lanes(k)] = state[p]
-                    now = decay_ref[k, i, n] * state[p] + dr[k] * b_in
+                    held[k, i, m] = state[p]
+                    decay = jnp.exp(st[k] * rate[p])
+                    decays[k, i, m] = decay
+                    now = decay * state[p] + dr[k] * b_in
                     new.append(now)
                     out[k] = out[k] + b_out * now
                     d_out = d_out + sd[k] * now
@@ -288,8 +290,8 @@
                 for k in range(HALVES):
                     p = m * HALVES + k
                     adjoint = b_out * sd[k] + incoming[p]
-                    passed = decay_ref[k, i, n] * adjoint
-                    pulled = passed * held[i, m, :, lanes(k)]
+                    passed = decays[k, i, m] * adjoint
+                    pulled = passed * held[k, i, m]
                     new_in.append(passed)
                     new_total.append(total[p] + pulled * st[k])
                     g_decay[k] = g_decay[k] + pulled * rate[p]
@@ -380,11 +382,11 @@
         ],
         out_specs=[
             stacked(STEPS, ROWS), tiled(TOK), tiled(TOK), stacked(STEPS, ROWS), stacked(STEPS, ROWS),
-            stacked(STEPS, N, ROWS), tiled(N, ROWS), tiled(N, ROWS), tiled(ROWS), whole(CTX, 2 * N, LANE),
+            tiled(N, ROWS), tiled(N, ROWS), tiled(ROWS), whole(CTX, 2 * N, LANE),
         ],
         out_shape=[
             f(ch // LANE, STEPS, ROWS, LANE), f(TOK, ch), f(TOK, ch), f(ch // LANE, STEPS, ROWS, LANE),
-            f(ch // LANE, STEPS, ROWS, LANE), f(ch // LANE, STEPS, N, ROWS, LANE),
+            f(ch // LANE, STEPS, ROWS, LANE),
             f(N, ROWS, ch), f(N, ROWS, ch),
             f(ROWS, ch), f(CTX, 2 * N, LANE),
         ],
@@ -419,7 +421,7 @@
         in_specs=[
             whole(TOK, R), whole(TOK, io.shape[1]), tiled(R), tiled(N), tiled(1),
             tiled(TOK), tiled(TOK), tiled(TOK), stacked(STEPS, ROWS), tiled(TOK), tiled(TOK),
-            stacked(STEPS, ROWS), stacked(STEPS, ROWS), stacked(STEPS, N, ROWS), tiled(N, ROWS), tiled(N, ROWS), tiled(ROWS), stacked(2 * N),
+            stacked(STEPS, ROWS), stacked(STEPS, ROWS), tiled(N, ROWS), tiled(N, ROWS), tiled(ROWS), stacked(2 * N),
         ],
         out_specs=[
             tiled(TOK), tiled(TOK), whole(TOK, WIDE), tiled(2, SIDE, 2, 2, 16), stacked(SMALL),
@@ -431,7 +433,8 @@
         scratch_shapes=[
             pltpu.VMEM((STEPS, 2 * N, ROWS, LANE), F32),
             pltpu.VMEM((STEPS, 2 * N, ROWS, LANE), F32),
-            pltpu.VMEM((STEPS, CHUNK, ROWS, TILE), F32),
+            pltpu.VMEM((HALVES, STEPS, CHUNK, ROWS, LANE), F32),
+            pltpu.VMEM((HALVES, STEPS, CHUNK, ROWS, LANE), F32),
         ]
         + [pltpu.VMEM((HALVES, STEPS, ROWS, LANE), F32)] * 3
         + [pltpu.VMEM((HALVES, TOK, LANE), F32)] * 3
@@ -545,13 +548,31 @@
     ]
 
 
-def sum_projected(u_ref, xt_ref, low_ref, io_ref, part_ref, *scratch):
+LOADS = 4
+
+
+def sum_projected(u_hbm, xt_hbm, low_ref, io_ref, part_ref, u_ref, xt_ref, load_sem, *scratch):
     low_part, io_part, low_land, io_land, low_all, io_all, wide, sum_send, sum_recv, all_send, all_recv = scratch
+    loads = []
+    wide_piece = u_ref.shape[1] // LOADS
+    for k in range(LOADS):
+        columns = slice(k * wide_piece, (k + 1) * wide_piece)
+        for m, (src, dst) in enumerate(((u_hbm, u_ref), (xt_hbm, xt_ref))):
+            loads.append(
+                pltpu.make_async_copy(src.at[:, columns], dst.at[:, columns], load_sem.at[m, k])
+            )
+            loads[-1].start()
     greet(others("ch", CH))
+    total = jnp.zeros((TOK, R + 2 * N), F32)
+    for k in range(LOADS):
+        columns = slice(k * wide_piece, (k + 1) * wide_piece)
+        loads[2 * k].wait()
+        loads[2 * k + 1].wait()
+        total = total + lax.dot_general(
+            u_ref[:, columns], xt_ref[:, columns], (((1,), (1,)), ((), ())), preferred_element_type=F32
+        )
     part_ref[:, R:] = jnp.zeros((TOK, LANE), F32)
-    part_ref[:, : R + 2 * N] = lax.dot_general(
-        u_ref[...], xt_ref[...], (((1,), (1,)), ((), ())), preferred_element_type=F32
-    )
+    part_ref[:, : R + 2 * N] = total
     prepare(part_ref, low_part, io_part)
     met(others("ch", CH))
     sums = sum_start(low_part, io_part, low_land, io_land, sum_send, sum_recv)
@@ -570,10 +591,14 @@
 def run_sum(u, xt):
     return pl.pallas_call(
         sum_projected,
-        in_specs=in_vmem(2),
+        in_specs=[pl.BlockSpec(memory_space=pl.ANY)] * 2,
         out_specs=in_vmem(2),
         out_shape=[jax.ShapeDtypeStruct((TOK, R), BF16), jax.ShapeDtypeStruct((TOK, LANE), F32)],
-        scratch_shapes=[pltpu.VMEM((TOK, WIDE), F32)] + sum_scratch(F32),
+        scratch_shapes=[
+            pltpu.VMEM((TOK, WIDE), F32), pltpu.VMEM(u.shape, BF16), pltpu.VMEM(xt.shape, BF16),
+            pltpu.SemaphoreType.DMA((2, LOADS)),
+        ]
+        + sum_scratch(F32),
         compiler_params=pltpu.CompilerParams(
             collective_id=0, has_side_effects=True, vmem_limit_bytes=VMEM_BYTES
         ),
@@ -719,20 +744,22 @@
 
 
 def tail(
-    part_ref, small_in, dgate_ref, step_grad, u_hbm, xw_hbm, dsig_hbm,
+    part_ref, small_in, dgate_hbm, grad_hbm, u_hbm, xw_hbm, dsig_hbm,
     hin_ref, hgate_ref, gx_ref, gstep_ref, gdecay_ref, gbias_ref, gskip_ref,
     low_part, io_part, low_land, io_land, low_all, io_all, wide, sum_send, sum_recv, all_send, all_recv,
     small_land, small_back, small_all, s_send, s_recv, t_send, t_recv,
     gate_land, in_out, in_land, hand_send, hand_recv, proj, proj_t, x_grad0, x_grad1,
-    u_ref, xw_ref, dsig_ref, load_sem, *scratch,
+    u_ref, xw_ref, dsig_ref, step_grad, load_sem, *scratch,
 ):
     rings = [scratch[k * RING : (k + 1) * RING] for k in range(4)]
     step_ring, x_ring = rings[:2], rings[2:]
+    grad_load = pltpu.make_async_copy(grad_hbm, step_grad, load_sem.at[3])
     step_grad = [step_grad.at[q] for q in range(2)]
     x_grad = [x_grad0, x_grad1]
     section = lax.axis_index("section")
     me = lax.axis_index("ctx")
     partners = others("ctx", CTX) + others("ch", CH) + [{"section": 1 - section}]
+    grad_load.start()
     greet(partners)
     loads = [
         pltpu.make_async_copy(src, dst, load_sem.at[k])
@@ -742,10 +769,11 @@
         load.start()
     prepare(part_ref, low_part, io_part)
     met(partners)
-    gate_copy = remote(dgate_ref, gate_land, hand_send.at[0], hand_recv.at[0], {"section": 1 - section})
+    gate_copy = remote(dgate_hbm, gate_land, hand_send.at[0], hand_recv.at[0], {"section": 1 - section})
     in_copy = remote(in_out, in_land, hand_send.at[1], hand_recv.at[1], {"section": 1 - section})
 
     sums = sum_start(low_part, io_part, low_land, io_land, sum_send, sum_recv)
+    grad_load.wait()
     first = plane_start(step_grad, step_ring)
 
     @pl.when(section == 1)
@@ -849,7 +877,7 @@
     b = lambda *s: jax.ShapeDtypeStruct(s, BF16)
     return pl.pallas_call(
         tail,
-        in_specs=in_vmem(4) + [pl.BlockSpec(memory_space=pl.ANY)] * 3,
+        in_specs=in_vmem(2) + [pl.BlockSpec(memory_space=pl.ANY)] * 5,
         out_specs=in_vmem(7),
         out_shape=[
             b(TOK, ch), b(TOK, ch), f(R + 2 * N, LANE), f(32, ch), f(N, ch), f(1, ch), f(1, ch),
@@ -862,7 +890,7 @@
         + [pltpu.VMEM((TOK, WIDE), BF16), pltpu.VMEM((WIDE, TOK), BF16)]
         + [pltpu.VMEM((SIDE, 2, 2, rows, LANE), BF16) for rows in X_ROWS]
         + [pltpu.VMEM(u.shape, BF16), pltpu.VMEM(xw.shape, BF16), pltpu.VMEM(dsig.shape, F32)]
-        + [pltpu.SemaphoreType.DMA((3,))]
+        + [pltpu.VMEM(step_grad.shape, BF16), pltpu.SemaphoreType.DMA((4,))]
         + ring_scratch((2, 16, 2048), (16, 1024)) * 2
         + ring_scratch((2, X_ROWS[0], LANE), (X_ROWS[0] // 2, LANE))
         + ring_scratch((2, X_ROWS[1], LANE), (X_ROWS[1] // 2, LANE)),

time: 153 us -> 150 us (0.980)
  Pallas kernels: 152 us -> 149 us
    pallas_call x2, Pallas kernels: 73.1 us -> 70 us  [the longest x1 42.8 us: run_tail(): pl.pallas_call(tail, in_specs=in_vmem(2) + [pl.BlockSpec(memory_space=pl....]
where the time goes in v5:
time: 150 us
  Pallas kernels  149 us (99%)
    pallas_call x1, Pallas kernels, run_tail(): pl.pallas_call(tail, in_specs=in_vmem(2) + [pl.BlockSpec(memory_space=pl....  42.8 us
    pallas_call x1, Pallas kernels, run_first(): pl.pallas_call(first_pass, grid=(ch // TILE,), in_specs=[whole(TOK, R), w...  40.1 us
    pallas_call x1, Pallas kernels, run_second(): pl.pallas_call(second_pass, grid=(ch // TILE,), in_specs=[whole(TOK, R),...  35.9 us
    pallas_call x1, Pallas kernels, run_sum(): pl.pallas_call(sum_projected, in_specs=[pl.BlockSpec(memory_space=pl.ANY)...  27.2 us

profile of v5, /device:TPU:2, one launch (start us, length us, event | category | flops | bytes accessed | tf_op | source)
XLA Modules:
  0.0 149.6 jit_solution(6173874205014709057)
XLA Ops:
  0.6 27.2 %sum_projected.1 = (bf16[192,512]{1,0:T(8,128)(2,1)}, f32[192,128]{1,0:T(8,128)}) custom-call(bf16[192,2048]{1,0:T(8,128)(2,1)} %bitcast.15, bf16[544,2048]{1,0:T(8,128)(2,1)} %bitcast.19), custom_call_target="tpu_custom_call" | custom-call | tf_op jit(solution)/shard_map/sum_projected/pallas_call | solution.py:592
  27.8 40.1 %first_pass.1 = (f32[16,24,8,128]{3,2,1,0:T(8,128)}, f32[192,2048]{1,0:T(8,128)}, f32[192,2048]{1,0:T(8,128)}, f32[16,24,8,128]{3,2,1,0:T(8,128)}, f32[16,24,8,1...) custom-call(bf16[192,512]{1,0:T(8,128)(2,1)} %get-tuple-element.37.l, ...), custom_call_target="tpu_custom_call" | custom-call | tf_op jit(solution)/shard_map/first_pass/pallas_call | solution.py:376
  67.9 35.9 %second_pass.1 = (bf16[192,2048]{1,0:T(8,128)(2,1)}, f32[192,2048]{1,0:T(8,128)}, f32[192,640]{1,0:T(8,128)}, bf16[2,4,2,2,16,2048]{5,4,3,2,1,0:T(8,128)(2,1)}, f32[16,24,128]{2,1,0:T(8,128)}) custom-call(bf16[192,512]{1,0:T(8,128)(2,1)} %get-tuple-element.37.low_ref, f32[192,128]{1,0:T(8,128)} %get-tuple-element.38.io_ref, bf16[512,2048]{1,0:T(8,128)(2,1)} %bitcast.22, ...), custom_call_target="tpu_custom_call" | custom-call | tf_op jit(solution)/shard_map/second_pass/pallas_call | solution.py:418
  103.8 42.8 %tail.1 = (bf16[192,2048]{1,0:T(8,128)(2,1)}, bf16[192,2048]{1,0:T(8,128)(2,1)}, f32[544,128]{1,0:T(8,128)}, f32[32,2048]{1,0:T(8,128)}, f32[16,2048]{1,0:T(8,12...) custom-call(f32[192,640]{1,0:T(8,128)} %get-tuple-element.48.part_ref, f32[16,24,128]{2,1,0:T(8,128)} %get-tuple-element.49.small_in, ...), custom_call_target="tpu_custom_call" | custom-call | tf_op jit(solution)/shard_map/tail/pallas_call | solution.py:878
  146.6 3.0 %finish.1 = (bf16[192,2048]{1,0:T(8,128)(2,1)}, bf16[192,2048]{1,0:T(8,128)(2,1)}, f32[544,128]{1,0:T(8,128)}, f32[32,2048]{1,0:T(8,128)}, f32[16,2048]{1,0:T(8,...) custom-call(bf16[192,2048]{1,0:T(8,128)(2,1)} %get-tuple-element.53.refs_0_, bf16[192,2048]{1,0:T(8,128)(2,1)} %get-tuple-element.54.refs_1_, ...), custom_call_target="tpu_custom_call" | custom-call | tf_op jit(solution)/shard_map/finish/pallas_call | solution.py:911

commit v6 on v5

--- a/solution.py
+++ b/solution.py
@@ -51,10 +51,6 @@
     return jnp.concatenate([by_token[k] for k in range(HALVES)], axis=1)
 
 
-def row_index():
-    return lax.broadcasted_iota(jnp.int32, (ROWS, LANE), 0)
-
-
 def spread_columns(io_ref, spread):
     def one(i, _):
         rows = io_ref[every(i), :]
@@ -70,15 +66,16 @@
     return rough * (2.0 - value * rough)
 
 
-def scan_rows(decay, value, reverse):
-    row = row_index()
-    for k in (1, 2, 4):
-        shift = ROWS - k if reverse else k
-        inside = row < ROWS - k if reverse else row >= k
-        value = value + decay * jnp.where(inside, pltpu.roll(value, shift, 0), 0.0)
-        if k < 4:
-            decay = decay * jnp.where(inside, pltpu.roll(decay, shift, 0), 1.0)
-    return value
+def block_rows(s):
+    return pl.ds(s, N, stride=ROWS)
+
+
+def scan_blocks(decays, values, out_ref, k, reverse):
+    state = jnp.zeros((N, LANE), F32)
+    for s in reversed(range(ROWS)) if reverse else range(ROWS):
+        out_ref[k, block_rows(s), :] = state
+        state = decays[k, block_rows(s), :] * state + values[k, block_rows(s), :]
+    return state
 
 
 def first_pass(
@@ -86,6 +83,7 @@
     step_ref, token_ref, sig_ref, drive, seed, entry_ref, exit_ref, bsum_ref, across_ref,
     spread, by_drive, by_seed, by_step_size, rates,
     pack, landed, back, result, send, recv, back_send, back_recv,
+    block_decay, block_end, block_start,
 ):
     tile = pl.program_id(0)
     last = pl.num_programs(0) - 1
@@ -107,8 +105,6 @@
     by_step(drive, step * u_ref[...].astype(F32), by_drive)
     by_step(seed, g_ref[...].astype(F32) * z * inverse(1.0 + jnp.exp(-z)), by_seed)
     rates[...] = -jnp.exp(dlog_ref[...])
-    row = row_index()
-
     total = jnp.zeros((ROWS, TILE), F32)
     for i in range(STEPS):
         total = total + jnp.concatenate([step_ref[k, i] for k in range(HALVES)], axis=1)
@@ -137,14 +133,16 @@
 
         zero = tuple(jnp.zeros((ROWS, LANE), F32) for _ in pairs)
         ones = tuple(jnp.ones((ROWS, LANE), F32) for _ in pairs)
-        state, decay, start = lax.fori_loop(0, STEPS, one, (zero, ones, zero), unroll=12)
+        state, decay, start = lax.fori_loop(0, STEPS, one, (zero, ones, zero), unroll=STEPS)
         for p, (n, k) in enumerate(pairs):
-            ends = scan_rows(decay[p], state[p], False)
-            starts = scan_rows(decay[p], start[p], True)
-            entry_ref[n, :, lanes(k)] = jnp.where(row >= 1, pltpu.roll(ends, 1, 0), 0.0)
-            exit_ref[n, :, lanes(k)] = jnp.where(row < ROWS - 1, pltpu.roll(starts, ROWS - 1, 0), 0.0)
-            pack[HALVES * tile + k, n : n + 1, :] = ends[ROWS - 1 :, :]
-            pack[HALVES * tile + k, N + n : N + n + 1, :] = starts[:1, :]
+            at = slice(n * ROWS, (n + 1) * ROWS)
+            block_decay[k, at, :] = decay[p]
+            block_end[k, at, :] = state[p]
+            block_start[k, at, :] = start[p]
+
+    for k in range(HALVES):
+        pack[HALVES * tile + k, :N, :] = scan_blocks(block_decay, block_end, entry_ref, k, False)
+        pack[HALVES * tile + k, N : 2 * N, :] = scan_blocks(block_decay, block_start, exit_ref, k, True)
 
     @pl.when(tile == 0)
     def _():
@@ -269,11 +267,11 @@
             return tuple(new)
 
         state = tuple(
-            entry_ref[n, :, lanes(k)]
+            entry_ref[k, n * ROWS : (n + 1) * ROWS, :]
             + jnp.exp(prior[:, lanes(k)] * rate[p]) * across_ref[k, n : n + 1, :]
             for p, (n, k) in enumerate(pairs)
         )
-        lax.fori_loop(0, STEPS, forward, state, unroll=8)
+        lax.fori_loop(0, STEPS, forward, state, unroll=STEPS)
 
         def backward(j, carry, c=c, numbers=numbers, rate=rate):
             incoming, total = carry
@@ -304,12 +302,12 @@
             return tuple(new_in), tuple(new_total)
 
         incoming = tuple(
-            exit_ref[n, :, lanes(k)]
+            exit_ref[k, n * ROWS : (n + 1) * ROWS, :]
             + jnp.exp(later[:, lanes(k)] * rate[p]) * across_ref[k, N + n : N + n + 1, :]
             for p, (n, k) in enumerate(pairs)
         )
         zero = tuple(jnp.zeros((ROWS, LANE), F32) for _ in pairs)
-        _, total = lax.fori_loop(0, STEPS, backward, (incoming, zero), unroll=8)
+        _, total = lax.fori_loop(0, STEPS, backward, (incoming, zero), unroll=STEPS)
         for p, (n, k) in enumerate(pairs):
             small_ref[k, n : n + 1, :] = (
                 jnp.sum(total[p], axis=0, keepdims=True) * rates[n : n + 1, lanes(k)]
@@ -382,12 +380,12 @@
         ],
         out_specs=[
             stacked(STEPS, ROWS), tiled(TOK), tiled(TOK), stacked(STEPS, ROWS), stacked(STEPS, ROWS),
-            tiled(N, ROWS), tiled(N, ROWS), tiled(ROWS), whole(CTX, 2 * N, LANE),
+            stacked(N * ROWS), stacked(N * ROWS), tiled(ROWS), whole(CTX, 2 * N, LANE),
         ],
         out_shape=[
             f(ch // LANE, STEPS, ROWS, LANE), f(TOK, ch), f(TOK, ch), f(ch // LANE, STEPS, ROWS, LANE),
             f(ch // LANE, STEPS, ROWS, LANE),
-            f(N, ROWS, ch), f(N, ROWS, ch),
+            f(ch // LANE, N * ROWS, LANE), f(ch // LANE, N * ROWS, LANE),
             f(ROWS, ch), f(CTX, 2 * N, LANE),
         ],
         scratch_shapes=[
@@ -404,7 +402,8 @@
             pltpu.SemaphoreType.DMA((CTX,)),
             pltpu.SemaphoreType.DMA((CTX - 1,)),
             pltpu.SemaphoreType.DMA((CTX - 1,)),
-        ],
+        ]
+        + [pltpu.VMEM((HALVES, N * ROWS, LANE), F32)] * 3,
         compiler_params=pltpu.CompilerParams(
             collective_id=1, has_side_effects=True, vmem_limit_bytes=VMEM_BYTES
         ),
@@ -421,7 +420,7 @@
         in_specs=[
             whole(TOK, R), whole(TOK, io.shape[1]), tiled(R), tiled(N), tiled(1),
             tiled(TOK), tiled(TOK), tiled(TOK), stacked(STEPS, ROWS), tiled(TOK), tiled(TOK),
-            stacked(STEPS, ROWS), stacked(STEPS, ROWS), tiled(N, ROWS), tiled(N, ROWS), tiled(ROWS), stacked(2 * N),
+            stacked(STEPS, ROWS), stacked(STEPS, ROWS), stacked(N * ROWS), stacked(N * ROWS), tiled(ROWS), stacked(2 * N),
         ],
         out_specs=[
             tiled(TOK), tiled(TOK), whole(TOK, WIDE), tiled(2, SIDE, 2, 2, 16), stacked(SMALL),
@@ -780,20 +779,9 @@
     def _():
         gate_copy.start()
 
+    shares = share_start(sums, part_ref, io_part, low_land, io_land, low_all, io_all, all_send, all_recv)
     small_there = spread_start(small_in, small_land, s_send, s_recv)
-    shares = share_start(sums, part_ref, io_part, low_land, io_land, low_all, io_all, all_send, all_recv)
     first = plane_middle(step_grad, step_ring, first)
-    for copy in small_there:
-        copy.wait_recv()
-    total = small_land[0]
-    for c in range(1, CTX):
-        total = total + small_land[c]
-    small_all[me] = total
-    small_home = []
-    for d, to in enumerate(others("ctx", CTX)):
-        small_home.append(remote(small_all.at[me], small_all.at[me], t_send.at[d], t_recv.at[d], to))
-        small_home[-1].start()
-
     share_finish(shares, low_all, io_all, wide)
     proj[...] = wide[...].astype(BF16)
     proj_t[...] = wide[...].T.astype(BF16)
@@ -833,9 +821,21 @@
         hin_ref[...] = jnp.zeros_like(hin_ref)
         hgate_ref[...] = jnp.zeros_like(hgate_ref)
 
+    first_x = plane_middle(x_grad, x_ring, first_x)
     turned = plane_turn(step_grad, step_ring, first, left_half)
-    first_x = plane_middle(x_grad, x_ring, first_x)
+    for copy in small_there:
+        copy.wait_recv()
+    total = small_land[0]
+    for c in range(1, CTX):
+        total = total + small_land[c]
+    small_all[me] = total
+    small_home = []
+    for d, to in enumerate(others("ctx", CTX)):
+        small_home.append(remote(small_all.at[me], small_all.at[me], t_send.at[d], t_recv.at[d], to))
+        small_home[-1].start()
+    turned_x = plane_turn(x_grad, x_ring, first_x, top_half)
     turned = plane_second_middle(step_ring, turned)
+    turned_x = plane_second_middle(x_ring, turned_x)
     for copy in small_home:
         copy.wait_recv()
     for c in range(CTX):
@@ -845,7 +845,6 @@
     for q, halves in enumerate(plane_finish(step_ring, turned)):
         for h in range(2):
             gstep_ref[q * 16 : (q + 1) * 16, h * 1024 : (h + 1) * 1024] = halves[h]
-    turned_x = plane_turn(x_grad, x_ring, first_x, top_half)
 
     @pl.when(section == 0)
     def _():
@@ -854,7 +853,6 @@
         hgate_ref[...] = gate_land[...]
         hin_ref[...] = in_land[...]
 
-    turned_x = plane_second_middle(x_ring, turned_x)
     for q, halves in enumerate(plane_finish(x_ring, turned_x)):
         for h in range(2):
             rows = X_ROWS[q] // 2

time: 150 us -> 145 us (0.967)
  Pallas kernels: 149 us -> 144 us
    pallas_call x1, Pallas kernels: 35.9 us -> 33.1 us  [run_second(): pl.pallas_call(second_pass, grid=(ch // TILE,), in_specs=[whole(TOK, R),...]
where the time goes in v6:
time: 145 us
  Pallas kernels  144 us (99%)
    pallas_call x1, Pallas kernels, run_tail(): pl.pallas_call(tail, in_specs=in_vmem(2) + [pl.BlockSpec(memory_space=pl....  42.1 us
    pallas_call x1, Pallas kernels, run_first(): pl.pallas_call(first_pass, grid=(ch // TILE,), in_specs=[whole(TOK, R), w...  38.7 us
    pallas_call x1, Pallas kernels, run_second(): pl.pallas_call(second_pass, grid=(ch // TILE,), in_specs=[whole(TOK, R),...  33.1 us
    pallas_call x1, Pallas kernels, run_sum(): pl.pallas_call(sum_projected, in_specs=[pl.BlockSpec(memory_space=pl.ANY)...  27.2 us
    pallas_call x1, Pallas kernels, run_finish(): pl.pallas_call(finish, in_specs=in_vmem(len(results)), out_specs=in_vmem(...  2.97 us

profile of v6, /device:TPU:2, one launch (start us, length us, event | category | flops | bytes accessed | tf_op | source)
XLA Modules:
  0.0 144.7 jit_solution(2178655104952335754)
XLA Ops:
  0.6 27.2 %sum_projected.1 = (bf16[192,512]{1,0:T(8,128)(2,1)}, f32[192,128]{1,0:T(8,128)}) custom-call(bf16[192,2048]{1,0:T(8,128)(2,1)} %bitcast.15, bf16[544,2048]{1,0:T(8,128)(2,1)} %bitcast.19), custom_call_target="tpu_custom_call" | custom-call | tf_op jit(solution)/shard_map/sum_projected/pallas_call | solution.py:591
  27.8 38.7 %first_pass.1 = (f32[16,24,8,128]{3,2,1,0:T(8,128)}, f32[192,2048]{1,0:T(8,128)}, f32[192,2048]{1,0:T(8,128)}, f32[16,24,8,128]{3,2,1,0:T(8,128)}, f32[16,24,8,1...) custom-call(bf16[192,512]{1,0:T(8,128)(2,1)} %get-tuple-element.37.l, ...), custom_call_target="tpu_custom_call" | custom-call | tf_op jit(solution)/shard_map/first_pass/pallas_call | solution.py:374
  66.5 33.1 %second_pass.1 = (bf16[192,2048]{1,0:T(8,128)(2,1)}, f32[192,2048]{1,0:T(8,128)}, f32[192,640]{1,0:T(8,128)}, bf16[2,4,2,2,16,2048]{5,4,3,2,1,0:T(8,128)(2,1)}, f32[16,24,128]{2,1,0:T(8,128)}) custom-call(bf16[192,512]{1,0:T(8,128)(2,1)} %get-tuple-element.37.low_ref, f32[192,128]{1,0:T(8,128)} %get-tuple-element.38.io_ref, bf16[512,2048]{1,0:T(8,128)(2,1)} %bitcast.22, ...), custom_call_target="tpu_custom_call" | custom-call | tf_op jit(solution)/shard_map/second_pass/pallas_call | solution.py:417
  99.6 42.1 %tail.1 = (bf16[192,2048]{1,0:T(8,128)(2,1)}, bf16[192,2048]{1,0:T(8,128)(2,1)}, f32[544,128]{1,0:T(8,128)}, f32[32,2048]{1,0:T(8,128)}, f32[16,2048]{1,0:T(8,12...) custom-call(f32[192,640]{1,0:T(8,128)} %get-tuple-element.48.part_ref, f32[16,24,128]{2,1,0:T(8,128)} %get-tuple-element.49.small_in, ...), custom_call_target="tpu_custom_call" | custom-call | tf_op jit(solution)/shard_map/tail/pallas_call | solution.py:876
  141.7 3.0 %finish.1 = (bf16[192,2048]{1,0:T(8,128)(2,1)}, bf16[192,2048]{1,0:T(8,128)(2,1)}, f32[544,128]{1,0:T(8,128)}, f32[32,2048]{1,0:T(8,128)}, f32[16,2048]{1,0:T(8,...) custom-call(bf16[192,2048]{1,0:T(8,128)(2,1)} %get-tuple-element.53.refs_0_, bf16[192,2048]{1,0:T(8,128)(2,1)} %get-tuple-element.54.refs_1_, ...), custom_call_target="tpu_custom_call" | custom-call | tf_op jit(solution)/shard_map/finish/pallas_call | solution.py:909

commit v7 on v6

--- a/solution.py
+++ b/solution.py
@@ -78,6 +78,17 @@
     return state
 
 
+def owner_of(tile, k):
+    x, y = tile // SIDE, tile % SIDE
+    return (x + 2 * k) * SIDE + (y + 2 * k) % SIDE
+
+
+def chunk_of(me):
+    x, y = me // SIDE, lax.rem(me, SIDE)
+    k = x // 2
+    return 2 * ((x - 2 * k) * SIDE + lax.rem(y + 2 * k, SIDE)) + k
+
+
 def first_pass(
     low_ref, io_ref, w_ref, bias_ref, dlog_ref, all_dlog_ref, u_ref, z_ref, g_ref,
     step_ref, token_ref, sig_ref, drive, seed, entry_ref, exit_ref, bsum_ref, across_ref,
@@ -148,37 +159,40 @@
     def _():
         met(others("ctx", CTX))
 
-    def chunk_to(c):
-        return remote(pack.at[c], landed.at[me], send.at[c], recv.at[me], {"ctx": c})
+    own = chunk_of(me)
+
+    def chunk_to(c, owner):
+        return remote(pack.at[c], landed.at[me], send.at[c], recv.at[me], {"ctx": owner})
 
     def chunk_from(c):
         return remote(pack.at[c], landed.at[c], send.at[c], recv.at[c], {"ctx": c})
 
     def answers():
         return [
-            remote(back.at[to["ctx"]], result.at[me], back_send.at[d], back_recv.at[d], to)
+            remote(back.at[to["ctx"]], result.at[own], back_send.at[d], back_recv.at[d], to)
             for d, to in enumerate(others("ctx", CTX))
         ]
 
     for k in range(HALVES):
         c = HALVES * tile + k
-
-        @pl.when(c != me)
+        owner = owner_of(tile, k)
+
+        @pl.when(owner != me)
         def _():
-            chunk_to(c).start()
-
-        @pl.when(c == me)
+            chunk_to(c, owner).start()
+
+        @pl.when(owner == me)
         def _():
-            landed[me] = pack[me]
-
-    @pl.when(tile == jnp.minimum(me // HALVES + 1, last))
+            landed[me] = pack[c]
+
+    @pl.when(tile == jnp.minimum(own // HALVES + 1, last))
     def _():
         for c in range(CTX):
             @pl.when(c != me)
             def _():
                 chunk_from(c).wait_recv()
 
-        mine = -jnp.exp(all_dlog_ref[:, pl.ds(pl.multiple_of(me * LANE, LANE), LANE)])
+        mine = -jnp.exp(all_dlog_ref[:, pl.ds(pl.multiple_of(own * LANE, LANE), LANE)])
         state = jnp.zeros((N, LANE), F32)
         adjoint = jnp.zeros((N, LANE), F32)
         for c in range(CTX):
@@ -187,7 +201,7 @@
             back[r, N:] = adjoint
             state = jnp.exp(landed[c, 2 * N : 2 * N + 1] * mine) * state + landed[c, :N]
             adjoint = jnp.exp(landed[r, 2 * N : 2 * N + 1] * mine) * adjoint + landed[r, N : 2 * N]
-        result[me] = back[me]
+        result[own] = back[me]
         for copy in answers():
             copy.start()
 
@@ -199,9 +213,11 @@
         for copy in answers():
             copy.wait_send()
         for c in range(CTX):
-            @pl.when(c != me)
+            owner = owner_of(c // HALVES, c % HALVES)
+
+            @pl.when(owner != me)
             def _():
-                chunk_to(c).wait_send()
+                chunk_to(c, owner).wait_send()
 
 
 def sum_before(value, reverse):
@@ -906,10 +922,18 @@
 
 
 def run_finish(*results):
+    def rows(r):
+        return pl.BlockSpec((r.shape[0] // SIDE, r.shape[1]), lambda j: (j, 0))
+
+    def columns(r):
+        return pl.BlockSpec((r.shape[0], r.shape[1] // SIDE), lambda j: (0, j))
+
+    specs = [rows(r) for r in results[:4]] + [columns(r) for r in results[4:]]
     return pl.pallas_call(
         finish,
-        in_specs=in_vmem(len(results)),
-        out_specs=in_vmem(len(results)),
+        grid=(SIDE,),
+        in_specs=specs,
+        out_specs=specs,
         out_shape=[jax.ShapeDtypeStruct(r.shape, r.dtype) for r in results],
         compiler_params=pltpu.CompilerParams(vmem_limit_bytes=VMEM_BYTES),
         name="finish",

time: 145 us -> 148 us (1.021)
  Pallas kernels: 144 us -> 147 us
    pallas_call x1, Pallas kernels: 42.1 us -> 44.3 us  [run_tail(): pl.pallas_call(tail, in_specs=in_vmem(2) + [pl.BlockSpec(memory_space=pl....]
where the time goes in v7:
time: 148 us; the launch traced here: 147 us
  Pallas kernels  147 us (99%)
    pallas_call x1, Pallas kernels, run_tail(): pl.pallas_call(tail, in_specs=in_vmem(2) + [pl.BlockSpec(memory_space=pl....  44.3 us
    pallas_call x1, Pallas kernels, run_first(): pl.pallas_call(first_pass, grid=(ch // TILE,), in_specs=[whole(TOK, R), w...  38.3 us
    pallas_call x1, Pallas kernels, run_second(): pl.pallas_call(second_pass, grid=(ch // TILE,), in_specs=[whole(TOK, R),...  33.1 us
    pallas_call x1, Pallas kernels, run_sum(): pl.pallas_call(sum_projected, in_specs=[pl.BlockSpec(memory_space=pl.ANY)...  27.2 us
    pallas_call x1, Pallas kernels, run_finish(): pl.pallas_call(finish, grid=(SIDE,), in_specs=specs, out_specs=specs, out...  3.84 us

profile of v7, /device:TPU:2, one launch (start us, length us, event | category | flops | bytes accessed | tf_op | source)
XLA Modules:
  0.0 147.4 jit_solution(241078345594738095)
XLA Ops:
  0.6 27.2 %sum_projected.1 = (bf16[192,512]{1,0:T(8,128)(2,1)}, f32[192,128]{1,0:T(8,128)}) custom-call(bf16[192,2048]{1,0:T(8,128)(2,1)} %bitcast.15, bf16[544,2048]{1,0:T(8,128)(2,1)} %bitcast.19), custom_call_target="tpu_custom_call" | custom-call | tf_op jit(solution)/shard_map/sum_projected/pallas_call | solution.py:607
  27.8 38.3 %first_pass.1 = (f32[16,24,8,128]{3,2,1,0:T(8,128)}, f32[192,2048]{1,0:T(8,128)}, f32[192,2048]{1,0:T(8,128)}, f32[16,24,8,128]{3,2,1,0:T(8,128)}, f32[16,24,8,1...) custom-call(bf16[192,512]{1,0:T(8,128)(2,1)} %get-tuple-element.37.l, ...), custom_call_target="tpu_custom_call" | custom-call | tf_op jit(solution)/shard_map/first_pass/pallas_call | solution.py:390
  66.1 33.1 %second_pass.1 = (bf16[192,2048]{1,0:T(8,128)(2,1)}, f32[192,2048]{1,0:T(8,128)}, f32[192,640]{1,0:T(8,128)}, bf16[2,4,2,2,16,2048]{5,4,3,2,1,0:T(8,128)(2,1)}, f32[16,24,128]{2,1,0:T(8,128)}) custom-call(bf16[192,512]{1,0:T(8,128)(2,1)} %get-tuple-element.37.low_ref, f32[192,128]{1,0:T(8,128)} %get-tuple-element.38.io_ref, bf16[512,2048]{1,0:T(8,128)(2,1)} %bitcast.22, ...), custom_call_target="tpu_custom_call" | custom-call | tf_op jit(solution)/shard_map/second_pass/pallas_call | solution.py:433
  99.3 44.3 %tail.1 = (bf16[192,2048]{1,0:T(8,128)(2,1)}, bf16[192,2048]{1,0:T(8,128)(2,1)}, f32[544,128]{1,0:T(8,128)}, f32[32,2048]{1,0:T(8,128)}, f32[16,2048]{1,0:T(8,12...) custom-call(f32[192,640]{1,0:T(8,128)} %get-tuple-element.48.part_ref, f32[16,24,128]{2,1,0:T(8,128)} %get-tuple-element.49.small_in, ...), custom_call_target="tpu_custom_call" | custom-call | tf_op jit(solution)/shard_map/tail/pallas_call | solution.py:892
  143.6 3.8 %finish.1 = (bf16[192,2048]{1,0:T(8,128)(2,1)}, bf16[192,2048]{1,0:T(8,128)(2,1)}, f32[544,128]{1,0:T(8,128)}, f32[32,2048]{1,0:T(8,128)}, f32[16,2048]{1,0:T(8,...) custom-call(bf16[192,2048]{1,0:T(8,128)(2,1)} %get-tuple-element.53.refs_0_, bf16[192,2048]{1,0:T(8,128)(2,1)} %get-tuple-element.54.refs_1_, ...), custom_call_target="tpu_custom_call" | custom-call | tf_op jit(solution)/shard_map/finish/pallas_call | solution.py:932

commit v8 on v6

--- a/solution.py
+++ b/solution.py
@@ -823,6 +823,7 @@
 
     first_x = plane_middle(x_grad, x_ring, first_x)
     turned = plane_turn(step_grad, step_ring, first, left_half)
+    turned_x = plane_turn(x_grad, x_ring, first_x, top_half)
     for copy in small_there:
         copy.wait_recv()
     total = small_land[0]
@@ -833,7 +834,6 @@
     for d, to in enumerate(others("ctx", CTX)):
         small_home.append(remote(small_all.at[me], small_all.at[me], t_send.at[d], t_recv.at[d], to))
         small_home[-1].start()
-    turned_x = plane_turn(x_grad, x_ring, first_x, top_half)
     turned = plane_second_middle(step_ring, turned)
     turned_x = plane_second_middle(x_ring, turned_x)
     for copy in small_home:

time: 145 us -> 145 us (level)
  no operation moved by 1% of the time
where the time goes in v8:
time: 145 us; the launch traced here: 144 us
  Pallas kernels  144 us (99%)
    pallas_call x1, Pallas kernels, run_tail(): pl.pallas_call(tail, in_specs=in_vmem(2) + [pl.BlockSpec(memory_space=pl....  41.6 us
    pallas_call x1, Pallas kernels, run_first(): pl.pallas_call(first_pass, grid=(ch // TILE,), in_specs=[whole(TOK, R), w...  38.7 us
    pallas_call x1, Pallas kernels, run_second(): pl.pallas_call(second_pass, grid=(ch // TILE,), in_specs=[whole(TOK, R),...  33.1 us
    pallas_call x1, Pallas kernels, run_sum(): pl.pallas_call(sum_projected, in_specs=[pl.BlockSpec(memory_space=pl.ANY)...  27.2 us
    pallas_call x1, Pallas kernels, run_finish(): pl.pallas_call(finish, in_specs=in_vmem(len(results)), out_specs=in_vmem(...  2.97 us

profile of v8, /device:TPU:2, one launch (start us, length us, event | category | flops | bytes accessed | tf_op | source)
XLA Modules:
  0.0 144.2 jit_solution(8326027041588717420)
XLA Ops:
  0.6 27.2 %sum_projected.1 = (bf16[192,512]{1,0:T(8,128)(2,1)}, f32[192,128]{1,0:T(8,128)}) custom-call(bf16[192,2048]{1,0:T(8,128)(2,1)} %bitcast.15, bf16[544,2048]{1,0:T(8,128)(2,1)} %bitcast.19), custom_call_target="tpu_custom_call" | custom-call | tf_op jit(solution)/shard_map/sum_projected/pallas_call | solution.py:591
  27.8 38.7 %first_pass.1 = (f32[16,24,8,128]{3,2,1,0:T(8,128)}, f32[192,2048]{1,0:T(8,128)}, f32[192,2048]{1,0:T(8,128)}, f32[16,24,8,128]{3,2,1,0:T(8,128)}, f32[16,24,8,1...) custom-call(bf16[192,512]{1,0:T(8,128)(2,1)} %get-tuple-element.37.l, ...), custom_call_target="tpu_custom_call" | custom-call | tf_op jit(solution)/shard_map/first_pass/pallas_call | solution.py:374
  66.5 33.1 %second_pass.1 = (bf16[192,2048]{1,0:T(8,128)(2,1)}, f32[192,2048]{1,0:T(8,128)}, f32[192,640]{1,0:T(8,128)}, bf16[2,4,2,2,16,2048]{5,4,3,2,1,0:T(8,128)(2,1)}, f32[16,24,128]{2,1,0:T(8,128)}) custom-call(bf16[192,512]{1,0:T(8,128)(2,1)} %get-tuple-element.37.low_ref, f32[192,128]{1,0:T(8,128)} %get-tuple-element.38.io_ref, bf16[512,2048]{1,0:T(8,128)(2,1)} %bitcast.22, ...), custom_call_target="tpu_custom_call" | custom-call | tf_op jit(solution)/shard_map/second_pass/pallas_call | solution.py:417
  99.6 41.6 %tail.1 = (bf16[192,2048]{1,0:T(8,128)(2,1)}, bf16[192,2048]{1,0:T(8,128)(2,1)}, f32[544,128]{1,0:T(8,128)}, f32[32,2048]{1,0:T(8,128)}, f32[16,2048]{1,0:T(8,12...) custom-call(f32[192,640]{1,0:T(8,128)} %get-tuple-element.48.part_ref, f32[16,24,128]{2,1,0:T(8,128)} %get-tuple-element.49.small_in, ...), custom_call_target="tpu_custom_call" | custom-call | tf_op jit(solution)/shard_map/tail/pallas_call | solution.py:876
  141.2 3.0 %finish.1 = (bf16[192,2048]{1,0:T(8,128)(2,1)}, bf16[192,2048]{1,0:T(8,128)(2,1)}, f32[544,128]{1,0:T(8,128)}, f32[32,2048]{1,0:T(8,128)}, f32[16,2048]{1,0:T(8,...) custom-call(bf16[192,2048]{1,0:T(8,128)(2,1)} %get-tuple-element.53.refs_0_, bf16[192,2048]{1,0:T(8,128)(2,1)} %get-tuple-element.54.refs_1_, ...), custom_call_target="tpu_custom_call" | custom-call | tf_op jit(solution)/shard_map/finish/pallas_call | solution.py:909
